TPU v7x, 128 devices: a whole 4x4x4 slice. The times are simulated.
128 devices in a mesh: dp: 16 (over y, z_lo, core), expert: 8 (over z_hi, x).
Axes of the slice: x: 4, y: 4, z: 4 (z_hi: 2, z_lo: 2; z = z_hi * 2 + z_lo), core: 2. Of those that a mesh axis runs over, the one named last changes fastest.
Arguments:
- queries: bfloat16 [2, 1024, 3072], P(None, 'dp', 'expert'), may hold values from -66 to 66
- prompt_kv: bfloat16 [2, 64, 256, 8, 256], P(None, 'dp', None, 'expert'), may hold values from -6 to 6
- new_kv: bfloat16 [2, 1024, 8, 256], P(None, 'dp', 'expert'), may hold values from -6 to 6
- prompt_slot: int32 [2, 64], replicated, may hold values from 0 to 63, each once within a row
- residual: bfloat16 [2, 1024, 6144], P(None, ('dp', 'expert')), may hold values from -6 to 6
- w_out: bfloat16 [3072, 6144], P('expert'), may hold values from -0.109375 to 0.109375
- norm_gain: float32 [6144], replicated, may hold values from 0.1 to 1.9
- w_router: bfloat16 [6144, 8], replicated, may hold values from -0.078125 to 0.078125
- routes: int32 [2, 1024, 2], P(None, ('dp', 'expert')), may hold values from 0 to 7, all different within a row; in each aligned block of 8 rows (0 to 7, 8 to 15, ..., all dimensions but the last counted through in order) at most 4 rows name the same one
- w_gate: bfloat16 [8, 6144, 8192], P('expert', None, 'dp'), may hold values from -0.078125 to 0.078125
- w_up: bfloat16 [8, 6144, 8192], P('expert', None, 'dp'), may hold values from -0.078125 to 0.078125
- w_down: bfloat16 [8, 8192, 6144], P('expert', 'dp'), may hold values from -0.0625 to 0.0625
Outputs:
- layer_out: bfloat16 [2, 1024, 6144], P(None, ('dp', 'expert'))
Inputs may be any that keep to these rules, and one draw needn't show every extreme that they name: Each step's row is a permutation; the slot of prompt_kv that holds group g's prompt lies on the index of dp given by prompt_slot // 4. `routes`: the two experts of a row differ. In each step the 8 rows of one device name one expert at most 4 times together, a bound that some block reaches.
All inputs are finite; a program needn't handle non-finite values.
Results may differ from a plain program's by a relative error of at most 0.017.
Values may be sent and summed in bfloat16 or wider, within the bound.
A program may use at most 128 MiB of HBM per device.

v0:
```python
import math

import jax
import jax.numpy as jnp
from jax import lax
from jax.sharding import PartitionSpec as P

HEAD = 128


neg_large = -1e30


def absorb(softmax_state, scores, values, validity):
    peak_old, total_old, summed_old = softmax_state
    peak_new = jnp.maximum(peak_old, jnp.max(scores, axis=-1))
    weights = jnp.exp(scores - peak_new[..., None])
    if validity is not None:
        weights = weights * validity[:, None, None].astype(jnp.float32)
    fading = jnp.exp(peak_old - peak_new)
    total_new = total_old * fading + jnp.sum(weights, axis=-1)
    summed_new = summed_old * fading[..., None] + jnp.einsum(
        "gak,gkd->gad", weights.astype(jnp.bfloat16), values, preferred_element_type=jnp.float32
    )
    return (peak_new, total_new, summed_new)


def body(
    queries,
    prompt_kv,
    new_kv,
    prompt_slot,
    residual,
    w_out,
    norm_gain,
    w_router,
    routes,
    w_gate,
    w_up,
    w_down,
):
    step_count = queries.shape[0]
    groups = queries.shape[1]
    per_kv = queries.shape[2] // HEAD
    factor = 1.0 / math.sqrt(HEAD)
    rows_moe = residual.shape[1]
    width = residual.shape[2]
    experts = lax.axis_size("expert")
    capacity = 2 * max(1, (2 * rows_moe + experts - 1) // experts)
    slot_count = experts * capacity
    expert_gate = w_gate[0]
    expert_up = w_up[0]
    expert_down = w_down[0]
    outputs = []
    for step_index in range(step_count):
        query_rows = queries[step_index].reshape(groups, per_kv, HEAD)
        slot_ids = prompt_slot[step_index]
        softmax_state = (
            jnp.full((groups, per_kv), neg_large, jnp.float32),
            jnp.zeros((groups, per_kv), jnp.float32),
            jnp.zeros((groups, per_kv, HEAD), jnp.float32),
        )
        stored = lax.all_gather(prompt_kv[step_index], "dp", axis=0, tiled=True)
        amount = stored.shape[0]
        validity = (slot_ids >= 0) & (slot_ids < amount)
        picked = jnp.take(stored[:, :, 0, :], jnp.clip(slot_ids, 0, amount - 1), axis=0)
        scores = (
            jnp.einsum(
                "gad,gpd->gap", query_rows, picked[..., :HEAD], preferred_element_type=jnp.float32
            )
            * factor
        )
        softmax_state = absorb(softmax_state, scores, picked[..., HEAD:], validity)
        recent_kv = jnp.transpose(new_kv[: step_index + 1, :, 0, :], (1, 0, 2))
        scores = (
            jnp.einsum(
                "gad,gsd->gas",
                query_rows,
                recent_kv[..., :HEAD],
                preferred_element_type=jnp.float32,
            )
            * factor
        )
        peak_all, total_all, summed_all = absorb(softmax_state, scores, recent_kv[..., HEAD:], None)
        attended = (
            (summed_all / total_all[..., None]).astype(jnp.bfloat16).reshape(groups, per_kv * HEAD)
        )
        mixed = residual[step_index].astype(jnp.float32) + lax.psum_scatter(
            jnp.dot(attended, w_out, preferred_element_type=jnp.float32).astype(jnp.bfloat16),
            "expert",
            scatter_dimension=0,
            tiled=True,
        ).astype(jnp.float32)
        spread = jnp.sqrt(jnp.mean(mixed * mixed, axis=-1, keepdims=True) + 1e-05)
        normed = (mixed / spread * norm_gain).astype(jnp.bfloat16)
        logits = jnp.dot(normed, w_router, preferred_element_type=jnp.float32)
        chosen_ids = routes[step_index]
        chosen = jnp.take_along_axis(logits, chosen_ids, axis=1)
        gates = jax.nn.sigmoid(chosen - chosen[:, ::-1])
        flat_ids = chosen_ids.reshape(-1)
        one_hot = (flat_ids[:, None] == jnp.arange(experts, dtype=jnp.int32)[None, :]).astype(
            jnp.int32
        )
        earlier = jnp.cumsum(one_hot, axis=0) - one_hot
        position = jnp.sum(earlier * one_hot, axis=1)
        target_slot = flat_ids * capacity + position
        selector = jnp.arange(slot_count, dtype=jnp.int32)[:, None] == target_slot[None, :]
        doubled = jnp.repeat(normed, 2, axis=0)
        outgoing = jnp.dot(
            selector.astype(jnp.bfloat16), doubled, preferred_element_type=jnp.float32
        )
        outgoing = outgoing.astype(jnp.bfloat16).reshape(experts, capacity, width)
        arrived = lax.all_to_all(
            outgoing, "expert", split_axis=0, concat_axis=0, tiled=True
        ).reshape(slot_count, width)
        block_rows = lax.all_gather(arrived, "dp", axis=0, tiled=True)
        gate_part = jnp.dot(block_rows, expert_gate, preferred_element_type=jnp.float32)
        up_part = jnp.dot(block_rows, expert_up, preferred_element_type=jnp.float32)
        hidden = (jax.nn.silu(gate_part) * up_part).astype(jnp.bfloat16)
        finished = lax.psum_scatter(
            jnp.dot(hidden, expert_down, preferred_element_type=jnp.float32).astype(jnp.bfloat16),
            "dp",
            scatter_dimension=0,
            tiled=True,
        ).astype(jnp.float32)
        returned = lax.all_to_all(
            finished.reshape(experts, capacity, width).astype(jnp.bfloat16),
            "expert",
            split_axis=0,
            concat_axis=0,
            tiled=True,
        ).astype(jnp.float32)
        per_pair = jnp.dot(
            selector.T.astype(jnp.float32),
            returned.reshape(slot_count, width),
            precision=lax.Precision.HIGHEST,
            preferred_element_type=jnp.float32,
        )
        per_pair = per_pair.reshape(rows_moe, 2, width)
        layer_rows = mixed + gates[:, 0:1] * per_pair[:, 0] + gates[:, 1:2] * per_pair[:, 1]
        outputs.append(layer_rows.astype(jnp.bfloat16))
    return jnp.stack(outputs)


def solution(mesh):
    placed = (
        P(None, "dp", "expert"),
        P(None, "dp", None, "expert", None),
        P(None, "dp", "expert", None),
        P(),
        P(None, ("dp", "expert"), None),
        P("expert", None),
        P(),
        P(),
        P(None, ("dp", "expert"), None),
        P("expert", None, "dp"),
        P("expert", None, "dp"),
        P("expert", "dp", None),
    )
    return jax.shard_map(
        body, mesh=mesh, in_specs=placed, out_specs=P(None, ("dp", "expert"), None), check_vma=False
    )
```

profile of v0, /device:TPU:1, one launch (start us, length us, event | category | flops | bytes accessed | tf_op | source)
XLA Modules:
  0.0 588.1 jit_solution(4933973983883294485)
XLA Ops:
  6.5 2.3 slice_bitcast_fusion.1
  8.9 0.7 all-gather.13.cloned.1.call-update
  9.7 0.8 fusion.120
  10.5 0.9 copy.109
  11.4 0.2 fusion.124
  11.8 0.8 slice_bitcast_fusion.6
  12.6 0.2 fusion.104
  12.8 0.8 compare_and_fusion.1
  13.7 0.8 fusion.117
  14.4 50.5 %all-gather.11.cloned.1.call-done = bf16[1,64,256,1,256]{4,2,3,0,1:T(8,128)(2,1)} async-done(((bf16[1,4,256,1,256]{4,2,3,0,1:T(8,128)(2,1)}), bf16[1,64,256,1,256]{4,2,3,0,1:T(8,128)(2,1)}) %all-gather.11.cloned.1.call-update) | async-done | bytes 8388624 | tf_op jit(solution)/shard_map/all_gather | solution.py:63
  64.9 8.9 %gather_fusion = bf16[64,256,256]{2,1,0:T(8,128)(2,1)} fusion(bf16[64,256,256]{2,1,0:T(8,128)(2,1)} %bitcast.180, s32[1024]{0:T(1024)S(1)} %pad_clamp_fusion.1), kind=kCustom, calls=%fused_computation.clone | custom fusion | bytes 16777472 | tf_op jit(solution)/shard_map/jit(_take)/gather | solution.py:66
  73.8 45.8 %all-gather.13.cloned.1.call-done = bf16[1,64,256,1,256]{4,2,3,0,1:T(8,128)(2,1)} async-done(((bf16[1,4,256,1,256]{4,2,3,0,1:T(8,128)(2,1)}), bf16[1,64,256,1,256]{4,2,3,0,1:T(8,128)(2,1)}) %all-gather.13.cloned.1.call-update) | async-done | bytes 8388624 | tf_op jit(solution)/shard_map/all_gather | solution.py:63
  119.6 8.9 %gather_fusion.2 = bf16[64,256,256]{2,1,0:T(8,128)(2,1)} fusion(bf16[64,256,256]{2,1,0:T(8,128)(2,1)} %bitcast.181, s32[1024]{0:T(1024)S(1)} %pad_clamp_fusion), kind=kCustom, calls=%fused_computation.2.clone | custom fusion | bytes 16777472 | tf_op jit(solution)/shard_map/jit(_take)/gather | solution.py:66
  128.5 9.4 %broadcast_select_fusion = (bf16[64,256,256]{2,1,0:T(8,128)(2,1)S(1)}, bf16[64,256,256]{2,1,0:T(8,128)(2,1)}) fusion(bf16[64,256,256]{2,1,0:T(8,128)(2,1)} %gather_fusion.2, pred[64]{0:T(512)(128)(4,1)S(1)} %get-tuple-element.44, bf16[64,256,256]{2,1,0:T(8,128)(2,1)} %gather_fusion, pred[64]{0:T(512)(128)(4,1)S(1)} %get-tuple-element.9), kind=kLoop, calls=%fused_computation.6 | loop fusion | flops 8388608 | bytes 33554560 | tf_op jit(solution)/shard_map/jit(_take)/select_n | solution.py:66
  138.0 3.2 copy-done.1
  141.2 1.3 fusion.123
  142.7 0.1 fusion.98
  142.8 0.3 fusion.100
  143.2 0.3 fusion.84
  143.9 2.9 fusion.63
  146.9 4.2 convolution_convert_fusion.2
  151.1 3.5 fusion.122
  154.8 0.3 fusion.82
  155.6 3.0 fusion.69
  158.6 4.2 convolution_convert_fusion.3
  163.2 0.2 select_reduce_fusion
  163.4 58.4 %reduce-scatter.9.cloned.1.call-done = bf16[8,6144]{1,0:T(8,128)(2,1)} async-done(((bf16[64,6144]{1,0:T(8,128)(2,1)}), bf16[8,6144]{1,0:T(8,128)(2,1)}) %reduce-scatter.9.cloned.1.call-update) | async-done | bytes 98320 | tf_op jit(solution)/shard_map/reduce_scatter | solution.py:88
  221.8 74.5 %reduce-scatter.5.cloned.1.call-done = bf16[8,6144]{1,0:T(8,128)(2,1)} async-done(((bf16[64,6144]{1,0:T(8,128)(2,1)}), bf16[8,6144]{1,0:T(8,128)(2,1)}) %reduce-scatter.5.cloned.1.call-update) | async-done | bytes 98320 | tf_op jit(solution)/shard_map/reduce_scatter | solution.py:88
  296.4 1.1 multiply_reduce_fusion.1
  297.6 1.1 multiply_convert_fusion.1
  298.6 0.1 broadcast_in_dim.14
  298.8 0.2 convolution_convert_fusion.4
  299.1 0.1 reshape.258
  299.2 12.6 %all_to_all.20 = bf16[8,4,6144]{2,1,0:T(4,128)(2,1)S(1)} all-to-all(bf16[8,4,6144]{2,1,0:T(4,128)(2,1)S(1)} %reshape.258), channel_id=1, replica_groups=mesh['dp'=16,'expert'=8] {'expert'}, dimensions={0} | all-to-all | bytes 786432 | tf_op jit(solution)/shard_map/all_to_all | solution.py:113
  311.8 0.9 reshape.259
  313.1 0.2 select_reduce_fusion.1
  313.5 0.2 convolution_convert_fusion.5
  313.7 0.1 reshape.253
  313.9 10.9 %all_to_all.21 = bf16[8,4,6144]{2,1,0:T(4,128)(2,1)S(1)} all-to-all(bf16[8,4,6144]{2,1,0:T(4,128)(2,1)S(1)} %reshape.253), channel_id=1, replica_groups=mesh['dp'=16,'expert'=8] {'expert'}, dimensions={0} | all-to-all | bytes 786432 | tf_op jit(solution)/shard_map/all_to_all | solution.py:113
  324.7 0.9 reshape.254
  325.6 0.2 reduce-scatter.11.cloned.1.call-start
  325.8 31.2 %all-gather.9.cloned.1.call-done = bf16[512,6144]{1,0:T(8,128)(2,1)} async-done(((bf16[32,6144]{1,0:T(8,128)(2,1)}), bf16[512,6144]{1,0:T(8,128)(2,1)}) %all-gather.9.cloned.1.call-update) | async-done | bytes 6291472 | tf_op jit(solution)/shard_map/all_gather | solution.py:116
  357.0 8.3 %fusion.6 = f32[512,512]{1,0:T(8,128)S(1)} fusion(bf16[512,6144]{1,0:T(8,128)(2,1)} %all-gather.9.cloned.1.call-done, bf16[1,6144,512]{2,1,0:T(8,128)(2,1)} %param.25), kind=kOutput, calls=%fused_computation.18 | convolution fusion | flops 3221225472 | bytes 13631488 | tf_op jit(solution)/shard_map/dot_general | solution.py:117
  365.4 6.4 %fusion.24 = bf16[512,512]{1,0:T(8,128)(2,1)S(1)} fusion(bf16[512,6144]{1,0:T(8,128)(2,1)S(1)} %copy-done.7, bf16[1,6144,512]{2,1,0:T(8,128)(2,1)} %param.26, f32[512,512]{1,0:T(8,128)S(1)} %fusion.6), kind=kOutput, calls=%fused_computation.32 | convolution fusion | flops 3222798336 | bytes 14155776 | tf_op jit(solution)/shard_map/dot_general | solution.py:118
  371.9 5.3 convolution_convert_fusion
  377.3 24.2 %all-gather.7.cloned.1.call-done = bf16[512,6144]{1,0:T(8,128)(2,1)} async-done(((bf16[32,6144]{1,0:T(8,128)(2,1)}), bf16[512,6144]{1,0:T(8,128)(2,1)}) %all-gather.7.cloned.1.call-update) | async-done | bytes 6291472 | tf_op jit(solution)/shard_map/all_gather | solution.py:116
  401.5 8.1 %fusion.8 = f32[512,512]{1,0:T(8,128)S(1)} fusion(bf16[512,6144]{1,0:T(8,128)(2,1)} %all-gather.7.cloned.1.call-done, bf16[1,6144,512]{2,1,0:T(8,128)(2,1)} %param.25), kind=kOutput, calls=%fused_computation.20 | convolution fusion | flops 3221225472 | bytes 13631488 | tf_op jit(solution)/shard_map/dot_general | solution.py:117
  409.6 6.4 %fusion.27 = bf16[512,512]{1,0:T(8,128)(2,1)S(1)} fusion(bf16[512,6144]{1,0:T(8,128)(2,1)S(1)} %copy-done.8, bf16[1,6144,512]{2,1,0:T(8,128)(2,1)} %param.26, f32[512,512]{1,0:T(8,128)S(1)} %fusion.8), kind=kOutput, calls=%fused_computation.33 | convolution fusion | flops 3222798336 | bytes 14155776 | tf_op jit(solution)/shard_map/dot_general | solution.py:118
  416.0 5.4 convolution_convert_fusion.1
  422.0 0.2 fusion.125
  422.1 0.7 gather_fusion.1
  423.0 0.2 fusion.126
  423.1 0.7 gather_fusion.3
  424.0 57.0 %reduce-scatter.11.cloned.1.call-done = bf16[32,6144]{1,0:T(8,128)(2,1)} async-done(((bf16[512,6144]{1,0:T(8,128)(2,1)}), bf16[32,6144]{1,0:T(8,128)(2,1)}) %reduce-scatter.11.cloned.1.call-update) | async-done | bytes 393232 | tf_op jit(solution)/shard_map/reduce_scatter | solution.py:120
  481.0 1.9 convert_element_type.147
  483.0 6.1 %all-to-all-start.3 = ((bf16[8,4,6144]{2,1,0:T(4,128)(2,1)}), bf16[8,4,6144]{2,1,0:T(4,128)(2,1)S(1)}, u32[]{:S(2)}, u32[]{:S(2)}) async-start(bf16[8,4,6144]{2,1,0:T(4,128)(2,1)} %convert_element_type.147), calls=%async_computation.7 | async-start | bytes 786432 | tf_op jit(solution)/shard_map/all_to_all | solution.py:126
  489.1 73.0 %reduce-scatter.7.cloned.1.call-done = bf16[32,6144]{1,0:T(8,128)(2,1)} async-done(((bf16[512,6144]{1,0:T(8,128)(2,1)}), bf16[32,6144]{1,0:T(8,128)(2,1)}) %reduce-scatter.7.cloned.1.call-update) | async-done | bytes 393232 | tf_op jit(solution)/shard_map/reduce_scatter | solution.py:120
  562.1 1.9 convert_element_type.131
  564.0 6.4 %all-to-all-start.1 = ((bf16[8,4,6144]{2,1,0:T(4,128)(2,1)}), bf16[8,4,6144]{2,1,0:T(4,128)(2,1)S(1)}, u32[]{:S(2)}, u32[]{:S(2)}) async-start(bf16[8,4,6144]{2,1,0:T(4,128)(2,1)} %convert_element_type.131), calls=%async_computation.3 | async-start | bytes 786432 | tf_op jit(solution)/shard_map/all_to_all | solution.py:126
  570.5 0.2 fusion.111
  570.7 9.4 %all-to-all-done.1 = bf16[8,4,6144]{2,1,0:T(4,128)(2,1)S(1)} async-done(((bf16[8,4,6144]{2,1,0:T(4,128)(2,1)}), bf16[8,4,6144]{2,1,0:T(4,128)(2,1)S(1)}, u32[]{:S(2)}, u32[]{:S(2)}) %all-to-all-start.1) | async-done | bytes 393248 | tf_op jit(solution)/shard_map/all_to_all | solution.py:126
  580.2 0.2 fusion.113
  580.4 0.1 fusion.92
  580.5 0.7 pad_maximum_fusion
  (106 shorter events, 4.0 us)
Async XLA Ops:
  6.5 415.4 %copy-start = (bf16[6144,8]{0,1:T(8,128)(2,1)S(1)}, bf16[6144,8]{0,1:T(8,128)(2,1)}, u32[]{:S(2)}) copy-start(bf16[6144,8]{0,1:T(8,128)(2,1)} %param.23) | copy-start | bytes 294916
  6.5 58.3 %all-gather.11.cloned.1.call-start = ((), (), s32[]{:S(2)}) async-start(), calls=%async_computation.14 | async-start | bytes 8912896 | tf_op jit(solution)/shard_map/all_gather | solution.py:63
  8.9 110.7 %all-gather.13.cloned.1.call-start = ((), (), s32[]{:S(2)}) async-start(), calls=%async_computation.15 | async-start | bytes 8912896 | tf_op jit(solution)/shard_map/all_gather | solution.py:63
  9.6 212.2 %reduce-scatter.9.cloned.1.call-start = ((), (), s32[]{:S(2)}) async-start(), calls=%async_computation.11 | async-start | bytes 884736 | tf_op jit(solution)/shard_map/reduce_scatter | solution.py:88
  138.0 3.2 copy-start.1
  151.1 145.3 %reduce-scatter.5.cloned.1.call-start = ((), (), s32[]{:S(2)}) async-start(), calls=%async_computation.8 | async-start | bytes 884736 | tf_op jit(solution)/shard_map/reduce_scatter | solution.py:88
  155.6 7.3 %copy-start.6 = (s32[2,8,2]{1,2,0:T(2,128)S(1)}, s32[2,8,2]{1,2,0:T(2,128)}, u32[]{:S(2)}) copy-start(s32[2,8,2]{1,2,0:T(2,128)} %param.24) | copy-start | bytes 388
  155.6 140.8 %copy-start.2 = (bf16[2,8,6144]{2,1,0:T(8,128)(2,1)S(1)}, bf16[2,8,6144]{2,1,0:T(8,128)(2,1)}, u32[]{:S(2)}) copy-start(bf16[2,8,6144]{2,1,0:T(8,128)(2,1)} %param.20) | copy-start | bytes 589828
  155.6 142.0 %copy-start.5 = (f32[6144]{0:T(1024)S(1)}, f32[6144]{0:T(1024)}, u32[]{:S(2)}) copy-start(f32[6144]{0:T(1024)} %param.22) | copy-start | bytes 73732
  162.9 194.2 %all-gather.9.cloned.1.call-start = ((), (), s32[]{:S(2)}) async-start(), calls=%async_computation.12 | async-start | bytes 6684672 | tf_op jit(solution)/shard_map/all_gather | solution.py:116
  312.7 88.7 %all-gather.7.cloned.1.call-start = ((), (), s32[]{:S(2)}) async-start(), calls=%async_computation.9 | async-start | bytes 6684672 | tf_op jit(solution)/shard_map/all_gather | solution.py:116
  325.6 155.4 %reduce-scatter.11.cloned.1.call-start = ((), (), s32[]{:S(2)}) async-start(), calls=%async_computation.13 | async-start | bytes 6684672 | tf_op jit(solution)/shard_map/reduce_scatter | solution.py:120
  357.0 8.3 %copy-start.7 = (bf16[512,6144]{1,0:T(8,128)(2,1)S(1)}, bf16[512,6144]{1,0:T(8,128)(2,1)}, u32[]{:S(2)}) copy-start(bf16[512,6144]{1,0:T(8,128)(2,1)} %all-gather.9.cloned.1.call-done) | copy-start | bytes 18874372
  357.0 14.8 %slice-start = ((s8[6291456]{0:T(1024)(128)(4,1)}), s8[4194304]{0:T(1024)(128)(4,1)S(1)}, s32[]{:S(2)}) async-start(s8[6291456]{0:T(1024)(128)(4,1)} %bitcast.186), calls=%async_computation.16 | async-start | bytes 8388608
  365.4 6.5 %slice-start.1 = ((s8[6291456]{0:T(1024)(128)(4,1)}), s8[2097152]{0:T(1024)(128)(4,1)S(1)}, s32[]{:S(2)}) async-start(s8[6291456]{0:T(1024)(128)(4,1)} %bitcast.186), calls=%async_computation.17 | async-start | bytes 4194304
  377.2 184.9 %reduce-scatter.7.cloned.1.call-start = ((), (), s32[]{:S(2)}) async-start(), calls=%async_computation.10 | async-start | bytes 6684672 | tf_op jit(solution)/shard_map/reduce_scatter | solution.py:120
  401.5 8.1 %copy-start.8 = (bf16[512,6144]{1,0:T(8,128)(2,1)S(1)}, bf16[512,6144]{1,0:T(8,128)(2,1)}, u32[]{:S(2)}) copy-start(bf16[512,6144]{1,0:T(8,128)(2,1)} %all-gather.7.cloned.1.call-done) | copy-start | bytes 18874372
  401.5 14.5 %slice-start.2 = ((s8[6291456]{0:T(1024)(128)(4,1)}), s8[4194304]{0:T(1024)(128)(4,1)S(1)}, s32[]{:S(2)}) async-start(s8[6291456]{0:T(1024)(128)(4,1)} %bitcast.188), calls=%async_computation.18 | async-start | bytes 8388608
  409.6 6.4 %slice-start.3 = ((s8[6291456]{0:T(1024)(128)(4,1)}), s8[2097152]{0:T(1024)(128)(4,1)S(1)}, s32[]{:S(2)}) async-start(s8[6291456]{0:T(1024)(128)(4,1)} %bitcast.188), calls=%async_computation.19 | async-start | bytes 4194304
  422.8 157.6 %copy-start.3 = (bf16[8,6144]{1,0:T(8,128)(2,1)S(1)}, bf16[8,6144]{1,0:T(8,128)(2,1)}, u32[]{:S(2)}) copy-start(bf16[8,6144]{1,0:T(8,128)(2,1)} %reduce-scatter.9.cloned.1.call-done) | copy-start | bytes 294916
  422.8 157.6 %copy-start.4 = (bf16[8,6144]{1,0:T(8,128)(2,1)S(1)}, bf16[8,6144]{1,0:T(8,128)(2,1)}, u32[]{:S(2)}) copy-start(bf16[8,6144]{1,0:T(8,128)(2,1)} %reduce-scatter.5.cloned.1.call-done) | copy-start | bytes 294916
  483.0 81.0 %all-to-all-start.3 = ((bf16[8,4,6144]{2,1,0:T(4,128)(2,1)}), bf16[8,4,6144]{2,1,0:T(4,128)(2,1)S(1)}, u32[]{:S(2)}, u32[]{:S(2)}) async-start(bf16[8,4,6144]{2,1,0:T(4,128)(2,1)} %convert_element_type.147), calls=%async_computation.7 | async-start | bytes 786432 | tf_op jit(solution)/shard_map/all_to_all | solution.py:126
  564.0 16.1 %all-to-all-start.1 = ((bf16[8,4,6144]{2,1,0:T(4,128)(2,1)}), bf16[8,4,6144]{2,1,0:T(4,128)(2,1)S(1)}, u32[]{:S(2)}, u32[]{:S(2)}) async-start(bf16[8,4,6144]{2,1,0:T(4,128)(2,1)} %convert_element_type.131), calls=%async_computation.3 | async-start | bytes 786432 | tf_op jit(solution)/shard_map/all_to_all | solution.py:126
Sparse Core Ops, SparseCore 0:
  9.1 55.7 all-gather.10
  66.6 52.9 all-gather.12
  151.2 70.5 reduce-scatter.8
  225.3 71.0 reduce-scatter.4
  312.9 44.1 all-gather.8
  358.6 42.8 all-gather.6
  403.9 77.1 reduce-scatter.10
  483.5 78.5 reduce-scatter.6
where the time goes:
time: 589 us; the launch traced here: 588 us
  waiting for transfers between devices  425 us (72%)
  matrix products  60.9 us (10%)
  local copies, waits for them, and re-layouts  36.2 us (6%)
  blocking collectives  23.5 us (4%)
  other arithmetic  15.7 us (3%)
  between operations  14 us (2%)
  starting transfers between devices  13 us (2%)
    reduce_scatter x2, waiting for transfers between devices, body(): lax.psum_scatter(jnp.dot(attended, w_out, preferred_element_type=jnp.floa...  133 us
    reduce_scatter x2, waiting for transfers between devices, body(): lax.psum_scatter(jnp.dot(hidden, expert_down, preferred_element_type=jnp....  130 us
    all_gather x2, waiting for transfers between devices, body(): stored = lax.all_gather(prompt_kv[step_index], 'dp', axis=0, tiled=True)  96.3 us
    all_gather x2, waiting for transfers between devices, body(): block_rows = lax.all_gather(arrived, 'dp', axis=0, tiled=True)  55.4 us
    all_to_all x2, blocking collectives, body(): lax.all_to_all(outgoing, 'expert', split_axis=0, concat_axis=0, tiled=True)  23.5 us
    gather x2, local copies, waits for them, and re-layouts, body(): jnp.take(stored[:, :, 0, :], jnp.clip(slot_ids, 0, amount - 1), axis=0)  17.8 us
    dot_general x2, matrix products, body(): jnp.dot(block_rows, expert_gate, preferred_element_type=jnp.float32)  16.4 us
    dot_general x2, matrix products, body(): up_part = jnp.dot(block_rows, expert_up, preferred_element_type=jnp.float32)  12.8 us
  transfers between devices with their start and end apart: 10, of which 9 were waited for; matrix products, arithmetic and copies ran while one was open for 13% of the time, Pallas kernels for 0%

commit v1 on v0

v1 whole, which is shorter than its diff:
```python
import math

import jax
import jax.numpy as jnp
from jax import lax
from jax.experimental import pallas as pl
from jax.experimental.pallas import tpu as pltpu
from jax.sharding import PartitionSpec as P

HEAD = 128
MESH = pl.DeviceIdType.MESH
BF = jnp.bfloat16
F32 = jnp.float32
NEG = -1e30

STEPS = 2
NDP = 16
NEX = 8
GROUPS = 64
D = 6144
HALF = D // 2
QUART = D // 4
FFD = 512
ROWS = 8
SLOTS = 32
TILE = 512


def iota(shape, dim):
    return lax.broadcasted_iota(jnp.int32, shape, dim)


def dot(a, b):
    return jnp.dot(a, b, preferred_element_type=F32)


def dot_nt(a, b):
    return lax.dot_general(a, b, (((1,), (1,)), ((), ())), preferred_element_type=F32)


def ones_where(cond):
    return jnp.where(cond, 1.0, 0.0).astype(BF)


def to_column(row):
    n = row.shape[1]
    eye = iota((n, n), 0) == iota((n, n), 1)
    return jnp.sum(jnp.where(eye, row, 0), axis=1, keepdims=True)


def loop(n, fn):
    lax.fori_loop(0, n, lambda i, c: (fn(i), c)[1], 0)


def tile_at(i, base=0):
    return pl.ds(pl.multiple_of(base + i * TILE, TILE), TILE)


def kernel(
    q_ref, pkv_ref, nkv_ref, slot_ref, res_ref, wo_hbm, gain_ref, wr_ref, routes_ref, wg_hbm, wu_hbm, wd_hbm,
    out_ref,
    wo, wg, wu, wd,
    qs_send, qs_recv, at_send, at_recv, op_send, op_recv, ds_send, ds_recv,
    mixed, nb, gat, held, acc_g, acc_u, hid, pair, transit, ysum, zsum, rt_send, rt_recv,
    w_sem, q_sem, a_sem, o_sem, d_sem, g_sem, r_sem, t_sem,
):
    dp = lax.axis_index("dp")
    ex = lax.axis_index("expert")
    y = dp // 4
    zl = (dp // 2) % 2
    core = dp % 2

    def at_dp(dy, flip_z=0, flip_c=0):
        yy = (y + dy) % 4
        zz = 1 - zl if flip_z else zl
        cc = 1 - core if flip_c else core
        return yy * 4 + zz * 2 + cc

    def remote(src, dst, sems, idx, to_dp, to_ex):
        return pltpu.make_async_remote_copy(
            src_ref=src,
            dst_ref=dst,
            send_sem=sems.at[(0, *idx)],
            recv_sem=sems.at[(1, *idx)],
            device_id=(to_dp, to_ex),
            device_id_type=MESH,
        )

    weights = [
        pltpu.make_async_copy(src, dst, w_sem.at[i])
        for i, (src, dst) in enumerate(((wo_hbm, wo), (wg_hbm, wg), (wu_hbm, wu), (wd_hbm, wd)))
    ]
    for copy in weights:
        copy.start()

    barrier = pltpu.get_barrier_semaphore()
    for d in range(1, NDP):
        pl.semaphore_signal(barrier, inc=1, device_id=((dp + d) % NDP, ex), device_id_type=MESH)
    for d in range(1, NEX):
        pl.semaphore_signal(barrier, inc=1, device_id=(dp, (ex + d) % NEX), device_id_type=MESH)

    row = iota((256, 128), 0)
    part_of = (row & 15) >> 2
    slot_rows = [slot_ref[t : t + 1, :] for t in range(STEPS)]
    r64 = iota((256, GROUPS), 0)
    want = 4 * (r64 >> 4) + (r64 & 3)

    def by_part(full):
        picked = jnp.zeros((256, HEAD), F32)
        for a in range(4):
            picked = jnp.where(part_of == a, full[:, a * HEAD : (a + 1) * HEAD], picked)
        return picked.astype(BF).reshape(NDP, 16, HEAD)

    for t in range(STEPS):
        order = ones_where(slot_rows[t] == want)
        first = dot(order, jnp.concatenate([q_ref[t], nkv_ref[t][:, :HEAD]], axis=1))
        qs_send[:, t, 0] = by_part(first)
        if t == 0:
            zero = jnp.zeros((GROUPS, 3 * HEAD), BF)
            second = jnp.concatenate([zero, nkv_ref[0][:, HEAD:]], axis=1)
        else:
            zero = jnp.zeros((GROUPS, HEAD), BF)
            second = jnp.concatenate([nkv_ref[0][:, :HEAD], zero, nkv_ref[0][:, HEAD:], nkv_ref[1][:, HEAD:]], axis=1)
        qs_send[:, t, 1] = by_part(dot(order, second))

    pl.semaphore_wait(barrier, NDP - 1 + NEX - 1)

    def spread_dp(send, recv, sems):
        return [remote(send.at[(dp + d) % NDP], recv.at[dp], sems, (d - 1,), (dp + d) % NDP, ex) for d in range(1, NDP)]

    q_copies = spread_dp(qs_send, qs_recv, q_sem)
    for copy in q_copies:
        copy.start()
    qs_recv[dp] = qs_send[dp]
    for copy in q_copies:
        copy.wait_recv()

    factor = 1.0 / math.sqrt(HEAD)
    r_s = iota((256, 1024), 0)
    own_prompt = (r_s & 3) == (iota((256, 1024), 1) >> 8)
    r_e, c_e = iota((256, 256), 0), iota((256, 256), 1)
    same_source = (r_e >> 4) == (c_e >> 4)

    def pick(block, base):
        return dot(ones_where(same_source & ((c_e & 15) == base + (r_e & 3))), block)

    for t in range(STEPS):
        first = qs_recv[:, t, 0].reshape(256, HEAD)
        second = qs_recv[:, t, 1].reshape(256, HEAD)
        stored = pkv_ref[t].reshape(1024, 2 * HEAD)
        scores = jnp.where(own_prompt, dot_nt(first, stored[:, :HEAD]) * factor, NEG)
        first_f = first.astype(F32)
        recent = [(pick(first, 12), pick(second, 12))]
        if t == 1:
            recent.append((pick(second, 0), pick(second, 8)))
        recent_scores = [jnp.sum(first_f * keys, axis=1, keepdims=True) * factor for keys, _ in recent]
        peak = jnp.max(scores, axis=1, keepdims=True)
        for s in recent_scores:
            peak = jnp.maximum(peak, s)
        weight = jnp.exp(scores - peak)
        total = jnp.sum(weight, axis=1, keepdims=True)
        summed = dot(weight.astype(BF), stored[:, HEAD:])
        for s, (_, values) in zip(recent_scores, recent):
            w = jnp.exp(s - peak)
            total = total + w
            summed = summed + w.astype(BF).astype(F32) * values
        at_send[:, t] = (summed / total).astype(BF).reshape(NDP, 16, HEAD)

    a_copies = spread_dp(at_send, at_recv, a_sem)
    for copy in a_copies:
        copy.start()
    at_recv[dp] = at_send[dp]
    for copy in a_copies:
        copy.wait_recv()

    c64 = iota((GROUPS, 256), 1)
    want_c = 4 * (c64 >> 4) + (c64 & 3)
    weights[0].wait()

    def spread_ex(send, recv, sems, t):
        return [
            remote(send.at[t, (ex + d) % NEX], recv.at[t, ex], sems, (t, d - 1), dp, (ex + d) % NEX)
            for d in range(1, NEX)
        ]

    o_copies = []
    for t in range(STEPS):
        back = at_recv[:, t].reshape(256, HEAD)
        back_f = back.astype(F32)
        parted = jnp.concatenate([jnp.where(part_of == a, back_f, 0.0).astype(BF) for a in range(3)], axis=1)
        order = ones_where(to_column(slot_rows[t]) == want_c)
        attended = dot(order, parted).astype(BF)

        def project(i, t=t, attended=attended):
            lo = dot(attended, wo[:, tile_at(i)])
            hi = dot(attended, wo[:, tile_at(i, HALF)])
            for e in range(NEX):
                both = jnp.concatenate([lo[e * 8 : e * 8 + 8], hi[e * 8 : e * 8 + 8]], axis=0)
                op_send[t, e, :, tile_at(i)] = both.astype(BF)

        loop(HALF // TILE, project)
        o_copies.append(spread_ex(op_send, op_recv, o_sem, t))
        for copy in o_copies[t]:
            copy.start()

    d_copies = [None, None]
    targets = [None, None]

    def mix(t):
        for copy in o_copies[t]:
            copy.wait_recv()

        def add(i, squares):
            total = op_send[t, ex, :, tile_at(i)].astype(F32)
            for d in range(1, NEX):
                total = total + op_recv[t, (ex + d) % NEX, :, tile_at(i)].astype(F32)
            lo = res_ref[t, :, tile_at(i)].astype(F32)
            hi = res_ref[t, :, tile_at(i, HALF)].astype(F32)
            total = total + jnp.concatenate([lo, hi], axis=0)
            mixed[t, :, tile_at(i)] = total
            return squares + total * total

        squares = lax.fori_loop(0, HALF // TILE, add, jnp.zeros((16, TILE), F32))
        per_half = jnp.sum(squares, axis=1, keepdims=True)
        inverse = 1.0 / jnp.sqrt((per_half[:8] + per_half[8:]) / D + 1e-05)
        inverse = jnp.concatenate([inverse, inverse], axis=0)

        def scale(i):
            lower = iota((16, TILE), 0) < 8
            gain = jnp.where(lower, gain_ref[:, tile_at(i)], gain_ref[:, tile_at(i, HALF)])
            nb[:, tile_at(i)] = (mixed[t, :, tile_at(i)] * inverse * gain).astype(BF)

        loop(HALF // TILE, scale)
        normed = nb[...].astype(F32)
        lo, hi = normed[:8], normed[8:]
        logits = dot_nt(lo.astype(BF), wr_ref[:, :HALF]) + dot_nt(hi.astype(BF), wr_ref[:, HALF:])
        rows = [routes_ref[t][k : k + 1, :] for k in range(2)]
        cols = [to_column(r) for r in rows]
        chosen = [jnp.sum(jnp.where(iota((8, 8), 1) == c, logits, 0.0), axis=1, keepdims=True) for c in cols]
        before = iota((8, 8), 1) < iota((8, 8), 0)
        cells = []
        for k in range(2):
            gat[t, k] = jnp.broadcast_to(jax.nn.sigmoid(chosen[k] - chosen[1 - k]), (8, 128))
            place = jnp.zeros((8, 1), jnp.int32)
            for other in rows:
                place = place + jnp.sum(jnp.where(before & (cols[k] == other), 1, 0), axis=1, keepdims=True)
            cells.append(cols[k] * 4 + place)
        targets[t] = cells
        c32 = iota((8, 32), 1) & 7
        cell_rows = [jnp.sum(jnp.where(c32 == iota((8, 32), 0), c, 0), axis=0, keepdims=True) for c in cells]
        r_d, c_d = iota((128, 32), 0), iota((128, 32), 1)
        cell = 4 * (r_d >> 4) + (r_d & 3)
        same_quarter = ((r_d & 15) >> 2) == (c_d >> 3)
        choose = ones_where(same_quarter & ((cell_rows[0] == cell) | (cell_rows[1] == cell)))
        quarters = jnp.concatenate([lo[:, :QUART], lo[:, QUART:], hi[:, :QUART], hi[:, QUART:]], axis=0).astype(BF)
        for i in range(QUART // TILE):
            cut = slice(i * TILE, (i + 1) * TILE)
            ds_send[t, :, :, cut] = dot(choose, quarters[:, cut]).astype(BF).reshape(NEX, 16, TILE)
        d_copies[t] = spread_ex(ds_send, ds_recv, d_sem, t)
        for copy in d_copies[t]:
            copy.start()

    r_u, c_u = iota((128, 128), 0), iota((128, 128), 1)
    unfold_matrix = ones_where(((r_u >> 5) == ((c_u & 15) >> 2)) & (((r_u & 31) >> 2) == (c_u >> 4)) & ((r_u & 3) == (c_u & 3)))
    fold_matrix = ones_where(((c_u >> 5) == ((r_u & 15) >> 2)) & (((c_u & 31) >> 2) == (r_u >> 4)) & ((c_u & 3) == (r_u & 3)))


    def unfold(t):
        for copy in d_copies[t]:
            copy.wait_recv()
        ds_recv[t, ex] = ds_send[t, ex]
        for i in range(QUART // TILE):
            cut = slice(i * TILE, (i + 1) * TILE)
            rows = dot(unfold_matrix, ds_recv[t, :, :, cut].reshape(128, TILE)).astype(BF)
            for quarter in range(4):
                start = quarter * QUART + i * TILE
                held[t, dp, :, start : start + TILE] = rows[quarter * SLOTS : (quarter + 1) * SLOTS]

    g_copies = [{}, {}]

    def give(t, kind, ref, to_dp):
        copy = remote(ref, ref, g_sem, (t, kind), to_dp, ex)
        copy.start()
        g_copies[t][kind] = copy

    def gather_own(t):
        own = held.at[t, dp]
        give(t, 0, own, at_dp(0, 1))
        give(t, 1, own, at_dp(1))
        give(t, 2, own, at_dp(3))
        give(t, 9, own, at_dp(0, 0, 1))

    def gather_z(t):
        g_copies[t][0].wait_recv()
        other = held.at[t, at_dp(0, 1)]
        give(t, 3, other, at_dp(1))
        give(t, 4, other, at_dp(3))
        give(t, 10, other, at_dp(0, 0, 1))

    def gather_near(t, plane):
        for kind, dy, to_dy, part in ((1, 3, 1, 0), (2, 1, 3, 16)):
            g_copies[t][kind + 2 * plane].wait_recv()
            source = at_dp(dy, plane)
            give(t, kind + 4 + 2 * plane, held.at[t, source, pl.ds(part, 16)], at_dp(to_dy))
            give(t, 9 + 2 * dy + plane, held.at[t, source], at_dp(0, 0, 1))

    def gather_far(t, plane):
        for kind in (5, 6):
            g_copies[t][kind + 2 * plane].wait_recv()
        give(t, 13 + plane, held.at[t, at_dp(2, plane)], at_dp(0, 0, 1))

    def gather_end(t):
        for kind in range(9, 17):
            g_copies[t][kind].wait_recv()

    def gate_up(t, first, last):
        if first == 0:
            acc_g[...] = jnp.zeros_like(acc_g)
            acc_u[...] = jnp.zeros_like(acc_u)

        def step(i):
            x = held[t, :, :, tile_at(i, first * TILE)].reshape(NDP * SLOTS, TILE)
            acc_g[...] += dot(x, wg[tile_at(i, first * TILE), :])
            acc_u[...] += dot(x, wu[tile_at(i, first * TILE), :])

        loop(last - first, step)

    def activate(t):
        hid[...] = (jax.nn.silu(acc_g[...]) * acc_u[...]).astype(BF)
        for copy in g_copies[t].values():
            copy.wait_send()

    def down(t, first, last):
        def step(i):
            y_part = dot(hid[...], wd[:, tile_at(i, first * TILE)])
            held[t, :, :, tile_at(i, first * TILE)] = y_part.astype(BF).reshape(NDP, SLOTS, TILE)

        loop(last - first, step)

    r_copies = [{}, {}]

    def pass_on(t, kind, src, dst, to_dp):
        copy = remote(src, dst, r_sem, (t, kind), to_dp, ex)
        copy.start()
        r_copies[t][kind] = copy

    def reduce_cores(t):
        for dy in (2, 1, 3, 0):
            for plane in range(2):
                kind = 2 * dy + plane
                pass_on(t, kind, held.at[t, at_dp(dy, plane, 1)], pair.at[t, kind], at_dp(0, 0, 1))

    def reduce_far(t):
        for plane in range(2):
            r_copies[t][4 + plane].wait_recv()
            there = at_dp(2, plane)

            def add(i, there=there, plane=plane):
                cut = tile_at(i)
                total = held[t, there, :, cut].astype(F32) + pair[t, 4 + plane, :, cut].astype(F32)
                held[t, there, :, cut] = total.astype(BF)

            loop(D // TILE, add)
            pass_on(t, 8 + plane, held.at[t, there, pl.ds(0, 16)], transit.at[t, 0, plane], at_dp(1))
            pass_on(t, 10 + plane, held.at[t, there, pl.ds(16, 16)], transit.at[t, 1, plane], at_dp(3))

    def reduce_near(t, way):
        dy = 1 if way == 0 else 3
        for plane in range(2):
            r_copies[t][2 * dy + plane].wait_recv()
            r_copies[t][8 + 2 * way + plane].wait_recv()
            there = at_dp(dy, plane)

            def add(i, there=there, plane=plane):
                cut = tile_at(i)
                total = held[t, there, :, cut].astype(F32) + pair[t, 2 * dy + plane, :, cut].astype(F32)
                moved = transit[t, way, plane, :, cut].astype(F32)
                if way == 0:
                    total = jnp.concatenate([total[:16] + moved, total[16:]], axis=0)
                else:
                    total = jnp.concatenate([total[:16], total[16:] + moved], axis=0)
                held[t, there, :, cut] = total.astype(BF)

            loop(D // TILE, add)
            pass_on(t, 12 + 2 * way + plane, held.at[t, there], ysum.at[t, way, plane], at_dp(dy))

    def here(t, plane, cut):
        total = held[t, at_dp(0, plane), :, cut].astype(F32) + pair[t, plane, :, cut].astype(F32)
        return total + ysum[t, 0, plane, :, cut].astype(F32) + ysum[t, 1, plane, :, cut].astype(F32)

    def reduce_here(t):
        for plane in (1, 0):
            for kind in (plane, 12 + plane, 14 + plane):
                r_copies[t][kind].wait_recv()
            if plane == 1:

                def add(i):
                    held[t, at_dp(0, 1), :, tile_at(i)] = here(t, 1, tile_at(i)).astype(BF)

                loop(D // TILE, add)
                pass_on(t, 16, held.at[t, at_dp(0, 1)], zsum.at[t], at_dp(0, 1))

    t_copies = [None, None]

    def finish(t):
        r_copies[t][16].wait_recv()
        for i in range(QUART // TILE):
            parts = []
            for quarter in range(4):
                cut = slice(quarter * QUART + i * TILE, quarter * QUART + (i + 1) * TILE)
                parts.append((here(t, 0, cut) + zsum[t, :, cut].astype(F32)).astype(BF))
            folded = dot(fold_matrix, jnp.concatenate(parts, axis=0)).astype(BF)
            rt_send[t, :, :, i * TILE : (i + 1) * TILE] = folded.reshape(NEX, 16, TILE)
        t_copies[t] = spread_ex(rt_send, rt_recv, t_sem, t)
        for copy in t_copies[t]:
            copy.start()
        rt_recv[t, ex] = rt_send[t, ex]

    def combine(t):
        for copy in t_copies[t]:
            copy.wait_recv()
        both = jnp.concatenate(targets[t], axis=0)
        c_c = iota((16, 128), 1)
        mine = both == 4 * (c_c >> 4) + (c_c & 3)
        gate0, gate1 = gat[t, 0][:, :1], gat[t, 1][:, :1]
        for i in range(QUART // TILE):
            came = rt_recv[t, :, :, i * TILE : (i + 1) * TILE].reshape(128, TILE)
            for quarter in range(4):
                out = dot(ones_where(mine & (((c_c & 15) >> 2) == quarter)), came)
                upper = (quarter // 2) * 8
                start = (quarter % 2) * QUART + i * TILE
                total = mixed[t, upper : upper + 8, start : start + TILE] + gate0 * out[:8] + gate1 * out[8:]
                place = quarter * QUART + i * TILE
                out_ref[t, :, place : place + TILE] = total.astype(BF)

    mix(0)
    unfold(0)
    gather_own(0)
    mix(1)
    gather_z(0)
    unfold(1)
    gather_own(1)
    gather_near(0, 0)
    gather_near(0, 1)
    gather_z(1)
    gather_far(0, 0)
    gather_far(0, 1)
    gather_end(0)
    for copy in weights[1:]:
        copy.wait()
    gate_up(0, 0, 4)
    gather_near(1, 0)
    gate_up(0, 4, 8)
    gather_near(1, 1)
    gate_up(0, 8, 12)
    activate(0)
    down(0, 0, 4)
    gather_far(1, 0)
    down(0, 4, 8)
    down(0, 8, 12)
    reduce_cores(0)
    gather_far(1, 1)
    gather_end(1)
    reduce_far(0)
    gate_up(1, 0, 6)
    reduce_near(0, 0)
    reduce_near(0, 1)
    gate_up(1, 6, 12)
    activate(1)
    down(1, 0, 6)
    reduce_here(0)
    down(1, 6, 12)
    reduce_cores(1)
    finish(0)
    reduce_far(1)
    reduce_near(1, 0)
    reduce_near(1, 1)
    reduce_here(1)
    combine(0)
    finish(1)
    combine(1)

    for copy in q_copies + a_copies:
        copy.wait_send()
    for t in range(STEPS):
        for copy in o_copies[t] + d_copies[t] + list(r_copies[t].values()) + t_copies[t]:
            copy.wait_send()


def body(queries, prompt_kv, new_kv, prompt_slot, residual, w_out, norm_gain, w_router, routes, w_gate, w_up, w_down):
    vmem = pl.BlockSpec(memory_space=pltpu.VMEM)
    hbm = pl.BlockSpec(memory_space=pl.ANY)
    dma = pltpu.SemaphoreType.DMA
    return pl.pallas_call(
        kernel,
        out_shape=jax.ShapeDtypeStruct((STEPS, ROWS, D), BF),
        in_specs=[vmem] * 5 + [hbm] + [vmem] * 3 + [hbm] * 3,
        out_specs=vmem,
        scratch_shapes=[
            pltpu.VMEM((3 * HEAD, D), BF),
            pltpu.VMEM((D, FFD), BF),
            pltpu.VMEM((D, FFD), BF),
            pltpu.VMEM((FFD, D), BF),
            pltpu.VMEM((NDP, STEPS, 2, 16, HEAD), BF),
            pltpu.VMEM((NDP, STEPS, 2, 16, HEAD), BF),
            pltpu.VMEM((NDP, STEPS, 16, HEAD), BF),
            pltpu.VMEM((NDP, STEPS, 16, HEAD), BF),
            pltpu.VMEM((STEPS, NEX, 16, HALF), BF),
            pltpu.VMEM((STEPS, NEX, 16, HALF), BF),
            pltpu.VMEM((STEPS, NEX, 16, QUART), BF),
            pltpu.VMEM((STEPS, NEX, 16, QUART), BF),
            pltpu.VMEM((STEPS, 16, HALF), F32),
            pltpu.VMEM((16, HALF), BF),
            pltpu.VMEM((STEPS, 2, 8, 128), F32),
            pltpu.VMEM((STEPS, NDP, SLOTS, D), BF),
            pltpu.VMEM((NDP * SLOTS, FFD), F32),
            pltpu.VMEM((NDP * SLOTS, FFD), F32),
            pltpu.VMEM((NDP * SLOTS, FFD), BF),
            pltpu.VMEM((STEPS, 8, SLOTS, D), BF),
            pltpu.VMEM((STEPS, 2, 2, 16, D), BF),
            pltpu.VMEM((STEPS, 2, 2, SLOTS, D), BF),
            pltpu.VMEM((STEPS, SLOTS, D), BF),
            pltpu.VMEM((STEPS, NEX, 16, QUART), BF),
            pltpu.VMEM((STEPS, NEX, 16, QUART), BF),
            dma((4,)),
            dma((2, NDP - 1)),
            dma((2, NDP - 1)),
            dma((2, STEPS, NEX - 1)),
            dma((2, STEPS, NEX - 1)),
            dma((2, STEPS, 17)),
            dma((2, STEPS, 17)),
            dma((2, STEPS, NEX - 1)),
        ],
        compiler_params=pltpu.CompilerParams(
            collective_id=0, has_side_effects=True, vmem_limit_bytes=63 * 1024 * 1024
        ),
    )(
        queries,
        prompt_kv[:, :, :, 0, :],
        new_kv[:, :, 0, :],
        prompt_slot,
        residual,
        w_out,
        norm_gain.reshape(1, D),
        w_router.T,
        jnp.transpose(routes, (0, 2, 1)),
        w_gate[0],
        w_up[0],
        w_down[0],
    )


def solution(mesh):
    placed = (
        P(None, "dp", "expert"),
        P(None, "dp", None, "expert", None),
        P(None, "dp", "expert", None),
        P(),
        P(None, ("dp", "expert"), None),
        P("expert", None),
        P(),
        P(),
        P(None, ("dp", "expert"), None),
        P("expert", None, "dp"),
        P("expert", None, "dp"),
        P("expert", "dp", None),
    )
    return jax.shard_map(body, mesh=mesh, in_specs=placed, out_specs=P(None, ("dp", "expert"), None), check_vma=False)
```

time: 589 us -> 205 us (0.35)
  waiting for transfers between devices: 425 us -> 0 us
  Pallas kernels: 0 us -> 201 us
  matrix products: 60.9 us -> 0 us
  local copies, waits for them, and re-layouts: 36.2 us -> 1.62 us
  blocking collectives: 23.5 us -> 0 us
  other arithmetic: 15.7 us -> 0 us
  between operations: 14 us -> 0.01 us
  starting transfers between devices: 13 us -> 0 us
    reduce_scatter x4 -> x0, waiting for transfers between devices: 263 us -> none  [the longest x2 133 us: body(): lax.psum_scatter(jnp.dot(attended, w_out, preferred_element_type=jnp.floa...]
    pallas_call x0 -> x1, Pallas kernels: none -> 201 us  [body(): pl.pallas_call(kernel, out_shape=jax.ShapeDtypeStruct((STEPS, ROWS, D), B...]
    all_gather x4 -> x0, waiting for transfers between devices: 152 us -> none  [the longest x2 96.3 us: body(): stored = lax.all_gather(prompt_kv[step_index], 'dp', axis=0, tiled=True)]
    dot_general x21 -> x0, matrix products: 60.9 us -> none  [the longest x2 16.4 us: body(): jnp.dot(block_rows, expert_gate, preferred_element_type=jnp.float32)]
    all_to_all x2 -> x0, blocking collectives: 23.5 us -> none  [body(): lax.all_to_all(outgoing, 'expert', split_axis=0, concat_axis=0, tiled=True)]
    gather x12 -> x0, local copies, waits for them, and re-layouts: 19.8 us -> none  [the longest x2 17.8 us: body(): jnp.take(stored[:, :, 0, :], jnp.clip(slot_ids, 0, amount - 1), axis=0)]
    all_to_all x2 -> x0, starting transfers between devices: 12.6 us -> none  [body(): lax.all_to_all(finished.reshape(experts, capacity, width).astype(jnp.bflo...]
    select_n x2 -> x0, other arithmetic: 9.45 us -> none  [the longest x1 9.45 us: body(): jnp.take(stored[:, :, 0, :], jnp.clip(slot_ids, 0, amount - 1), axis=0)]
  transfers between devices with their start and end apart: 10 -> 0, of which waited for: 9 -> 0; matrix products, arithmetic and copies ran while one was open for 13% -> 0% of each run, Pallas kernels for 0% -> 0%
where the time goes in v1:
time: 205 us; the launch traced here: 202 us
  Pallas kernels  201 us (98%)
    pallas_call x1, Pallas kernels, body(): pl.pallas_call(kernel, out_shape=jax.ShapeDtypeStruct((STEPS, ROWS, D), B...  201 us

profile of v1, /device:TPU:1, one launch (start us, length us, event | category | flops | bytes accessed | tf_op | source)
XLA Modules:
  0.0 202.5 jit_solution(2392200696820077787)
XLA Ops:
  0.0 200.8 %shard_map.118 = bf16[2,8,6144]{2,1,0:T(8,128)(2,1)} custom-call(bf16[2,64,384]{2,1,0:T(8,128)(2,1)} %q_ref.1, bf16[2,4,256,256]{3,2,1,0:T(8,128)(2,1)} %bitcast.11, bf16[2,64,256]{2,1,0:T(8,128)(2,1)} %bitcast.13, s32[2,64]{1,0:T(2,128)} %slot_ref.1, bf16[2,8,6144]{2,1,0:T(8,128)(2,1)} %res_ref.1, bf16[384,6144]{1,0:T(8,128)(2,1)} %wo_hbm.1, ...), custom_call_target="tpu_custom_call" | custom-call | tf_op jit(solution)/shard_map/pallas_call | solution.py:494
  200.8 1.6 copy.14

commit v2 on v1

--- a/solution.py
+++ b/solution.py
@@ -24,6 +24,7 @@
 ROWS = 8
 SLOTS = 32
 TILE = 512
+NA = 4096
 
 
 def iota(shape, dim):
@@ -61,7 +62,7 @@
     out_ref,
     wo, wg, wu, wd,
     qs_send, qs_recv, at_send, at_recv, op_send, op_recv, ds_send, ds_recv,
-    mixed, nb, gat, held, acc_g, acc_u, hid, pair, transit, ysum, zsum, rt_send, rt_recv,
+    mixed, nb, gat, held, acc_g, acc_u, hid, pair, transit, ysum, zsum, zcross, rt_send, rt_recv,
     w_sem, q_sem, a_sem, o_sem, d_sem, g_sem, r_sem, t_sem,
 ):
     dp = lax.axis_index("dp")
@@ -75,6 +76,21 @@
         zz = 1 - zl if flip_z else zl
         cc = 1 - core if flip_c else core
         return yy * 4 + zz * 2 + cc
+
+    to_arrive, to_leave = [], []
+
+    def start(copy):
+        copy.start()
+        to_arrive.append(copy)
+        to_leave.append(copy)
+
+    def arrived(copy):
+        copy.wait_recv()
+        to_arrive[:] = [c for c in to_arrive if c is not copy]
+
+    def left(copy):
+        copy.wait_send()
+        to_leave[:] = [c for c in to_leave if c is not copy]
 
     def remote(src, dst, sems, idx, to_dp, to_ex):
         return pltpu.make_async_remote_copy(
@@ -114,26 +130,28 @@
     for t in range(STEPS):
         order = ones_where(slot_rows[t] == want)
         first = dot(order, jnp.concatenate([q_ref[t], nkv_ref[t][:, :HEAD]], axis=1))
-        qs_send[:, t, 0] = by_part(first)
+        qs_send[t, :, 0] = by_part(first)
         if t == 0:
             zero = jnp.zeros((GROUPS, 3 * HEAD), BF)
             second = jnp.concatenate([zero, nkv_ref[0][:, HEAD:]], axis=1)
         else:
             zero = jnp.zeros((GROUPS, HEAD), BF)
             second = jnp.concatenate([nkv_ref[0][:, :HEAD], zero, nkv_ref[0][:, HEAD:], nkv_ref[1][:, HEAD:]], axis=1)
-        qs_send[:, t, 1] = by_part(dot(order, second))
+        qs_send[t, :, 1] = by_part(dot(order, second))
 
     pl.semaphore_wait(barrier, NDP - 1 + NEX - 1)
 
-    def spread_dp(send, recv, sems):
-        return [remote(send.at[(dp + d) % NDP], recv.at[dp], sems, (d - 1,), (dp + d) % NDP, ex) for d in range(1, NDP)]
-
-    q_copies = spread_dp(qs_send, qs_recv, q_sem)
-    for copy in q_copies:
-        copy.start()
-    qs_recv[dp] = qs_send[dp]
-    for copy in q_copies:
-        copy.wait_recv()
+    def spread_dp(send, recv, sems, t):
+        copies = []
+        for d in range(1, NDP):
+            to = (dp + d) % NDP
+            copies.append(remote(send.at[t, to], recv.at[t, dp], sems, (t, d - 1), to, ex))
+        for copy in copies:
+            start(copy)
+        recv[t, dp] = send[t, dp]
+        return copies
+
+    q_copies = [spread_dp(qs_send, qs_recv, q_sem, t) for t in range(STEPS)]
 
     factor = 1.0 / math.sqrt(HEAD)
     r_s = iota((256, 1024), 0)
@@ -144,9 +162,12 @@
     def pick(block, base):
         return dot(ones_where(same_source & ((c_e & 15) == base + (r_e & 3))), block)
 
+    a_copies = []
     for t in range(STEPS):
-        first = qs_recv[:, t, 0].reshape(256, HEAD)
-        second = qs_recv[:, t, 1].reshape(256, HEAD)
+        for copy in q_copies[t]:
+            arrived(copy)
+        first = qs_recv[t, :, 0].reshape(256, HEAD)
+        second = qs_recv[t, :, 1].reshape(256, HEAD)
         stored = pkv_ref[t].reshape(1024, 2 * HEAD)
         scores = jnp.where(own_prompt, dot_nt(first, stored[:, :HEAD]) * factor, NEG)
         first_f = first.astype(F32)
@@ -164,14 +185,8 @@
             w = jnp.exp(s - peak)
             total = total + w
             summed = summed + w.astype(BF).astype(F32) * values
-        at_send[:, t] = (summed / total).astype(BF).reshape(NDP, 16, HEAD)
-
-    a_copies = spread_dp(at_send, at_recv, a_sem)
-    for copy in a_copies:
-        copy.start()
-    at_recv[dp] = at_send[dp]
-    for copy in a_copies:
-        copy.wait_recv()
+        at_send[t] = (summed / total).astype(BF).reshape(NDP, 16, HEAD)
+        a_copies.append(spread_dp(at_send, at_recv, a_sem, t))
 
     c64 = iota((GROUPS, 256), 1)
     want_c = 4 * (c64 >> 4) + (c64 & 3)
@@ -185,7 +200,9 @@
 
     o_copies = []
     for t in range(STEPS):
-        back = at_recv[:, t].reshape(256, HEAD)
+        for copy in a_copies[t]:
+            arrived(copy)
+        back = at_recv[t].reshape(256, HEAD)
         back_f = back.astype(F32)
         parted = jnp.concatenate([jnp.where(part_of == a, back_f, 0.0).astype(BF) for a in range(3)], axis=1)
         order = ones_where(to_column(slot_rows[t]) == want_c)
@@ -201,14 +218,14 @@
         loop(HALF // TILE, project)
         o_copies.append(spread_ex(op_send, op_recv, o_sem, t))
         for copy in o_copies[t]:
-            copy.start()
+            start(copy)
 
     d_copies = [None, None]
     targets = [None, None]
 
     def mix(t):
         for copy in o_copies[t]:
-            copy.wait_recv()
+            arrived(copy)
 
         def add(i, squares):
             total = op_send[t, ex, :, tile_at(i)].astype(F32)
@@ -258,7 +275,7 @@
             ds_send[t, :, :, cut] = dot(choose, quarters[:, cut]).astype(BF).reshape(NEX, 16, TILE)
         d_copies[t] = spread_ex(ds_send, ds_recv, d_sem, t)
         for copy in d_copies[t]:
-            copy.start()
+            start(copy)
 
     r_u, c_u = iota((128, 128), 0), iota((128, 128), 1)
     unfold_matrix = ones_where(((r_u >> 5) == ((c_u & 15) >> 2)) & (((r_u & 31) >> 2) == (c_u >> 4)) & ((r_u & 3) == (c_u & 3)))
@@ -267,7 +284,7 @@
 
     def unfold(t):
         for copy in d_copies[t]:
-            copy.wait_recv()
+            arrived(copy)
         ds_recv[t, ex] = ds_send[t, ex]
         for i in range(QUART // TILE):
             cut = slice(i * TILE, (i + 1) * TILE)
@@ -276,42 +293,62 @@
                 start = quarter * QUART + i * TILE
                 held[t, dp, :, start : start + TILE] = rows[quarter * SLOTS : (quarter + 1) * SLOTS]
 
+    part_a, part_b = pl.ds(0, NA), pl.ds(NA, D - NA)
+    whole = slice(None)
+    lower, upper = pl.ds(0, 16), pl.ds(16, 16)
     g_copies = [{}, {}]
 
-    def give(t, kind, ref, to_dp):
-        copy = remote(ref, ref, g_sem, (t, kind), to_dp, ex)
-        copy.start()
-        g_copies[t][kind] = copy
+    def give(t, name, device, to_dp, rows=whole, columns=whole):
+        ref = held.at[t, device, rows, columns]
+        copy = remote(ref, ref, g_sem, (t, len(g_copies[t])), to_dp, ex)
+        start(copy)
+        g_copies[t][name] = copy
+
+    def got(t, *names):
+        for name in names:
+            arrived(g_copies[t][name])
+
+    def to_core(t, dy, plane):
+        give(t, f"core{dy}{plane}", at_dp(dy, plane), at_dp(0, 0, 1))
 
     def gather_own(t):
-        own = held.at[t, dp]
-        give(t, 0, own, at_dp(0, 1))
-        give(t, 1, own, at_dp(1))
-        give(t, 2, own, at_dp(3))
-        give(t, 9, own, at_dp(0, 0, 1))
+        give(t, "z", dp, at_dp(0, 1), columns=part_a)
+        give(t, "up0", dp, at_dp(1))
+        give(t, "down0", dp, at_dp(3))
+        give(t, "cross0", dp, at_dp(0, 1), columns=part_b)
+        to_core(t, 0, 0)
 
     def gather_z(t):
-        g_copies[t][0].wait_recv()
-        other = held.at[t, at_dp(0, 1)]
-        give(t, 3, other, at_dp(1))
-        give(t, 4, other, at_dp(3))
-        give(t, 10, other, at_dp(0, 0, 1))
+        got(t, "z")
+        give(t, "up1", at_dp(0, 1), at_dp(1), columns=part_a)
+        give(t, "down1", at_dp(0, 1), at_dp(3), columns=part_a)
 
     def gather_near(t, plane):
-        for kind, dy, to_dy, part in ((1, 3, 1, 0), (2, 1, 3, 16)):
-            g_copies[t][kind + 2 * plane].wait_recv()
-            source = at_dp(dy, plane)
-            give(t, kind + 4 + 2 * plane, held.at[t, source, pl.ds(part, 16)], at_dp(to_dy))
-            give(t, 9 + 2 * dy + plane, held.at[t, source], at_dp(0, 0, 1))
-
-    def gather_far(t, plane):
-        for kind in (5, 6):
-            g_copies[t][kind + 2 * plane].wait_recv()
-        give(t, 13 + plane, held.at[t, at_dp(2, plane)], at_dp(0, 0, 1))
+        columns = part_a if plane else whole
+        got(t, f"up{plane}")
+        give(t, f"far_up{plane}", at_dp(3, plane), at_dp(1), lower, columns)
+        got(t, f"down{plane}")
+        give(t, f"far_down{plane}", at_dp(1, plane), at_dp(3), upper, columns)
+        if plane == 0:
+            for dy in (3, 1):
+                give(t, f"cross{dy}", at_dp(dy), at_dp(0, 1), columns=part_b)
+                to_core(t, dy, 0)
+
+    def gather_far(t):
+        got(t, "far_up0", "far_down0")
+        give(t, "cross2", at_dp(2), at_dp(0, 1), columns=part_b)
+        to_core(t, 2, 0)
+
+    def gather_cross(t, *dys):
+        for dy in dys:
+            if dy == 2:
+                got(t, "far_up1", "far_down1")
+            got(t, f"cross{dy}")
+            to_core(t, dy, 1)
 
     def gather_end(t):
-        for kind in range(9, 17):
-            g_copies[t][kind].wait_recv()
+        for dy in (0, 1, 3, 2):
+            got(t, f"core{dy}0", f"core{dy}1")
 
     def gate_up(t, first, last):
         if first == 0:
@@ -328,7 +365,7 @@
     def activate(t):
         hid[...] = (jax.nn.silu(acc_g[...]) * acc_u[...]).astype(BF)
         for copy in g_copies[t].values():
-            copy.wait_send()
+            left(copy)
 
     def down(t, first, last):
         def step(i):
@@ -339,86 +376,136 @@
 
     r_copies = [{}, {}]
 
-    def pass_on(t, kind, src, dst, to_dp):
-        copy = remote(src, dst, r_sem, (t, kind), to_dp, ex)
-        copy.start()
-        r_copies[t][kind] = copy
+    def pass_on(t, name, src, dst, to_dp):
+        copy = remote(src, dst, r_sem, (t, len(r_copies[t])), to_dp, ex)
+        start(copy)
+        r_copies[t][name] = copy
+
+    def came(t, *names):
+        for name in names:
+            arrived(r_copies[t][name])
+
+    def part(t, dy, plane, rows, cut):
+        return held[t, at_dp(dy, plane), rows, cut].astype(F32) + pair[t, 2 * dy + plane, rows, cut].astype(F32)
+
+    def crossed(t, dy, rows, i):
+        return zcross[t, dy, rows, tile_at(i)].astype(F32)
+
+    def over_a(t, dy, plane, rows, *more):
+        def step(i):
+            cut = tile_at(i)
+            total = part(t, dy, plane, rows, cut)
+            for term in more:
+                total = total + term(cut)
+            held[t, at_dp(dy, plane), rows, cut] = total.astype(BF)
+
+        loop(NA // TILE, step)
+
+    def over_b(t, dy, plane, rows, *more):
+        def step(i):
+            cut = tile_at(i, NA)
+            total = part(t, dy, plane, rows, cut)
+            if plane == 0:
+                total = total + crossed(t, dy, rows, i)
+            for term in more:
+                total = total + term(cut)
+            held[t, at_dp(dy, plane), rows, cut] = total.astype(BF)
+
+        loop((D - NA) // TILE, step)
 
     def reduce_cores(t):
+        for dy, plane in ((2, 1), (1, 1), (3, 1), (0, 1), (2, 0), (1, 0), (3, 0), (0, 0)):
+            kind = 2 * dy + plane
+            pass_on(t, f"core{dy}{plane}", held.at[t, at_dp(dy, plane, 1)], pair.at[t, kind], at_dp(0, 0, 1))
+
+    def send_transit(t, plane):
+        columns = part_a if plane else whole
+        for way, to_dy, rows in ((0, 1, lower), (1, 3, upper)):
+            src = held.at[t, at_dp(2, plane), rows, columns]
+            dst = transit.at[t, way, plane, whole, columns]
+            pass_on(t, f"transit{way}{plane}", src, dst, at_dp(to_dy))
+
+    def reduce_cross(t):
         for dy in (2, 1, 3, 0):
-            for plane in range(2):
-                kind = 2 * dy + plane
-                pass_on(t, kind, held.at[t, at_dp(dy, plane, 1)], pair.at[t, kind], at_dp(0, 0, 1))
+            came(t, f"core{dy}1")
+            over_b(t, dy, 1, whole)
+            pass_on(t, f"cross{dy}", held.at[t, at_dp(dy, 1), whole, part_b], zcross.at[t, dy], at_dp(0, 1))
+            if dy == 2:
+                over_a(t, 2, 1, whole)
+                send_transit(t, 1)
+
+    def send_sum(t, name, way, plane, rows):
+        columns = part_a if plane else whole
+        dy = 1 if way == 0 else 3
+        src = held.at[t, at_dp(dy, plane), rows, columns]
+        pass_on(t, f"{name}{way}{plane}", src, ysum.at[t, way, plane, rows, columns], at_dp(dy))
+
+    def reduce_free1(t):
+        for way, dy, rows in ((0, 1, upper), (1, 3, lower)):
+            over_a(t, dy, 1, rows)
+            send_sum(t, "free", way, 1, rows)
 
     def reduce_far(t):
-        for plane in range(2):
-            r_copies[t][4 + plane].wait_recv()
-            there = at_dp(2, plane)
-
-            def add(i, there=there, plane=plane):
-                cut = tile_at(i)
-                total = held[t, there, :, cut].astype(F32) + pair[t, 4 + plane, :, cut].astype(F32)
-                held[t, there, :, cut] = total.astype(BF)
-
-            loop(D // TILE, add)
-            pass_on(t, 8 + plane, held.at[t, there, pl.ds(0, 16)], transit.at[t, 0, plane], at_dp(1))
-            pass_on(t, 10 + plane, held.at[t, there, pl.ds(16, 16)], transit.at[t, 1, plane], at_dp(3))
-
-    def reduce_near(t, way):
-        dy = 1 if way == 0 else 3
-        for plane in range(2):
-            r_copies[t][2 * dy + plane].wait_recv()
-            r_copies[t][8 + 2 * way + plane].wait_recv()
-            there = at_dp(dy, plane)
-
-            def add(i, there=there, plane=plane):
-                cut = tile_at(i)
-                total = held[t, there, :, cut].astype(F32) + pair[t, 2 * dy + plane, :, cut].astype(F32)
-                moved = transit[t, way, plane, :, cut].astype(F32)
-                if way == 0:
-                    total = jnp.concatenate([total[:16] + moved, total[16:]], axis=0)
-                else:
-                    total = jnp.concatenate([total[:16], total[16:] + moved], axis=0)
-                held[t, there, :, cut] = total.astype(BF)
-
-            loop(D // TILE, add)
-            pass_on(t, 12 + 2 * way + plane, held.at[t, there], ysum.at[t, way, plane], at_dp(dy))
-
-    def here(t, plane, cut):
-        total = held[t, at_dp(0, plane), :, cut].astype(F32) + pair[t, plane, :, cut].astype(F32)
-        return total + ysum[t, 0, plane, :, cut].astype(F32) + ysum[t, 1, plane, :, cut].astype(F32)
+        came(t, "core20", "cross2")
+        over_a(t, 2, 0, whole)
+        over_b(t, 2, 0, whole)
+        send_transit(t, 0)
+
+    def reduce_free0(t):
+        for way, dy, rows in ((0, 1, upper), (1, 3, lower)):
+            came(t, f"core{dy}0", f"cross{dy}")
+            over_a(t, dy, 0, rows)
+            over_b(t, dy, 0, rows)
+            send_sum(t, "free", way, 0, rows)
+
+    def reduce_bound(t, plane):
+        for way, dy, rows in ((0, 1, lower), (1, 3, upper)):
+            came(t, f"transit{way}{plane}")
+
+            def moved(cut, way=way):
+                return transit[t, way, plane, :, cut].astype(F32)
+
+            over_a(t, dy, plane, rows, moved)
+            if plane == 0:
+                over_b(t, dy, plane, rows, moved)
+            send_sum(t, "bound", way, plane, rows)
+
+    def around(t, plane, cut):
+        return ysum[t, 0, plane, :, cut].astype(F32) + ysum[t, 1, plane, :, cut].astype(F32)
+
+    def came_around(t, plane):
+        came(t, *(f"{name}{way}{plane}" for name in ("free", "bound") for way in range(2)))
 
     def reduce_here(t):
-        for plane in (1, 0):
-            for kind in (plane, 12 + plane, 14 + plane):
-                r_copies[t][kind].wait_recv()
-            if plane == 1:
-
-                def add(i):
-                    held[t, at_dp(0, 1), :, tile_at(i)] = here(t, 1, tile_at(i)).astype(BF)
-
-                loop(D // TILE, add)
-                pass_on(t, 16, held.at[t, at_dp(0, 1)], zsum.at[t], at_dp(0, 1))
+        came_around(t, 1)
+        over_a(t, 0, 1, whole, lambda cut: around(t, 1, cut))
+        pass_on(t, "z", held.at[t, at_dp(0, 1), whole, part_a], zsum.at[t], at_dp(0, 1))
 
     t_copies = [None, None]
 
     def finish(t):
-        r_copies[t][16].wait_recv()
+        came_around(t, 0)
+        came(t, "core00", "cross0", "z")
         for i in range(QUART // TILE):
             parts = []
             for quarter in range(4):
                 cut = slice(quarter * QUART + i * TILE, quarter * QUART + (i + 1) * TILE)
-                parts.append((here(t, 0, cut) + zsum[t, :, cut].astype(F32)).astype(BF))
+                total = part(t, 0, 0, whole, cut) + around(t, 0, cut)
+                if cut.start < NA:
+                    total = total + zsum[t, :, cut].astype(F32)
+                else:
+                    total = total + zcross[t, 0, :, cut.start - NA : cut.stop - NA].astype(F32)
+                parts.append(total.astype(BF))
             folded = dot(fold_matrix, jnp.concatenate(parts, axis=0)).astype(BF)
             rt_send[t, :, :, i * TILE : (i + 1) * TILE] = folded.reshape(NEX, 16, TILE)
         t_copies[t] = spread_ex(rt_send, rt_recv, t_sem, t)
         for copy in t_copies[t]:
-            copy.start()
+            start(copy)
         rt_recv[t, ex] = rt_send[t, ex]
 
     def combine(t):
         for copy in t_copies[t]:
-            copy.wait_recv()
+            arrived(copy)
         both = jnp.concatenate(targets[t], axis=0)
         c_c = iota((16, 128), 1)
         mine = both == 4 * (c_c >> 4) + (c_c & 3)
@@ -438,53 +525,58 @@
     gather_own(0)
     mix(1)
     gather_z(0)
+    gather_near(0, 0)
     unfold(1)
+    gather_near(0, 1)
     gather_own(1)
-    gather_near(0, 0)
-    gather_near(0, 1)
-    gather_z(1)
-    gather_far(0, 0)
-    gather_far(0, 1)
-    gather_end(0)
+    gather_cross(0, 0, 1, 3)
+    gather_far(0)
+    gather_cross(0, 2)
     for copy in weights[1:]:
         copy.wait()
-    gate_up(0, 0, 4)
+    gather_end(0)
+    gate_up(0, 0, 6)
+    gather_z(1)
+    gate_up(0, 6, 12)
     gather_near(1, 0)
-    gate_up(0, 4, 8)
+    activate(0)
+    down(0, 0, 6)
     gather_near(1, 1)
-    gate_up(0, 8, 12)
-    activate(0)
-    down(0, 0, 4)
-    gather_far(1, 0)
-    down(0, 4, 8)
-    down(0, 8, 12)
+    down(0, 6, 12)
     reduce_cores(0)
-    gather_far(1, 1)
+    gather_cross(1, 0, 1, 3)
+    reduce_cross(0)
+    reduce_free1(0)
+    gather_far(1)
+    reduce_far(0)
+    reduce_free0(0)
+    gather_cross(1, 2)
     gather_end(1)
-    reduce_far(0)
-    gate_up(1, 0, 6)
-    reduce_near(0, 0)
-    reduce_near(0, 1)
-    gate_up(1, 6, 12)
+    gate_up(1, 0, 4)
+    reduce_bound(0, 1)
+    gate_up(1, 4, 8)
+    reduce_bound(0, 0)
+    gate_up(1, 8, 12)
     activate(1)
-    down(1, 0, 6)
+    down(1, 0, 12)
+    reduce_cores(1)
     reduce_here(0)
-    down(1, 6, 12)
-    reduce_cores(1)
+    reduce_cross(1)
+    reduce_free1(1)
+    reduce_far(1)
+    reduce_free0(1)
     finish(0)
-    reduce_far(1)
-    reduce_near(1, 0)
-    reduce_near(1, 1)
+    reduce_bound(1, 1)
+    reduce_bound(1, 0)
+    combine(0)
     reduce_here(1)
-    combine(0)
     finish(1)
     combine(1)
 
-    for copy in q_copies + a_copies:
-        copy.wait_send()
-    for t in range(STEPS):
-        for copy in o_copies[t] + d_copies[t] + list(r_copies[t].values()) + t_copies[t]:
-            copy.wait_send()
+    for copy in list(to_arrive):
+        arrived(copy)
+    for copy in list(to_leave):
+        left(copy)
 
 
 def body(queries, prompt_kv, new_kv, prompt_slot, residual, w_out, norm_gain, w_router, routes, w_gate, w_up, w_down):
@@ -501,10 +593,10 @@
             pltpu.VMEM((D, FFD), BF),
             pltpu.VMEM((D, FFD), BF),
             pltpu.VMEM((FFD, D), BF),
-            pltpu.VMEM((NDP, STEPS, 2, 16, HEAD), BF),
-            pltpu.VMEM((NDP, STEPS, 2, 16, HEAD), BF),
-            pltpu.VMEM((NDP, STEPS, 16, HEAD), BF),
-            pltpu.VMEM((NDP, STEPS, 16, HEAD), BF),
+            pltpu.VMEM((STEPS, NDP, 2, 16, HEAD), BF),
+            pltpu.VMEM((STEPS, NDP, 2, 16, HEAD), BF),
+            pltpu.VMEM((STEPS, NDP, 16, HEAD), BF),
+            pltpu.VMEM((STEPS, NDP, 16, HEAD), BF),
             pltpu.VMEM((STEPS, NEX, 16, HALF), BF),
             pltpu.VMEM((STEPS, NEX, 16, HALF), BF),
             pltpu.VMEM((STEPS, NEX, 16, QUART), BF),
@@ -519,16 +611,17 @@
             pltpu.VMEM((STEPS, 8, SLOTS, D), BF),
             pltpu.VMEM((STEPS, 2, 2, 16, D), BF),
             pltpu.VMEM((STEPS, 2, 2, SLOTS, D), BF),
-            pltpu.VMEM((STEPS, SLOTS, D), BF),
+            pltpu.VMEM((STEPS, SLOTS, NA), BF),
+            pltpu.VMEM((STEPS, 4, SLOTS, D - NA), BF),
             pltpu.VMEM((STEPS, NEX, 16, QUART), BF),
             pltpu.VMEM((STEPS, NEX, 16, QUART), BF),
             dma((4,)),
-            dma((2, NDP - 1)),
-            dma((2, NDP - 1)),
+            dma((2, STEPS, NDP - 1)),
+            dma((2, STEPS, NDP - 1)),
             dma((2, STEPS, NEX - 1)),
             dma((2, STEPS, NEX - 1)),
-            dma((2, STEPS, 17)),
-            dma((2, STEPS, 17)),
+            dma((2, STEPS, 40)),
+            dma((2, STEPS, 40)),
             dma((2, STEPS, NEX - 1)),
         ],
         compiler_params=pltpu.CompilerParams(

time: 205 us -> 176 us (0.86)
  Pallas kernels: 201 us -> 171 us
    pallas_call x1, Pallas kernels: 201 us -> 171 us  [body(): pl.pallas_call(kernel, out_shape=jax.ShapeDtypeStruct((STEPS, ROWS, D), B...]
where the time goes in v2:
time: 176 us; the launch traced here: 173 us
  Pallas kernels  171 us (97%)
    pallas_call x1, Pallas kernels, body(): pl.pallas_call(kernel, out_shape=jax.ShapeDtypeStruct((STEPS, ROWS, D), B...  171 us

profile of v2, /device:TPU:1, one launch (start us, length us, event | category | flops | bytes accessed | tf_op | source)
XLA Modules:
  0.0 173.1 jit_solution(12814850884705776368)
XLA Ops:
  0.0 171.5 %shard_map.118 = bf16[2,8,6144]{2,1,0:T(8,128)(2,1)} custom-call(bf16[2,64,384]{2,1,0:T(8,128)(2,1)} %q_ref.1, bf16[2,4,256,256]{3,2,1,0:T(8,128)(2,1)} %bitcast.11, bf16[2,64,256]{2,1,0:T(8,128)(2,1)} %bitcast.13, s32[2,64]{1,0:T(2,128)} %slot_ref.1, bf16[2,8,6144]{2,1,0:T(8,128)(2,1)} %res_ref.1, bf16[384,6144]{1,0:T(8,128)(2,1)} %wo_hbm.1, ...), custom_call_target="tpu_custom_call" | custom-call | tf_op jit(solution)/shard_map/pallas_call | solution.py:586
  171.5 1.6 copy.14

commit v3 on v2

--- a/solution.py
+++ b/solution.py
@@ -24,7 +24,7 @@
 ROWS = 8
 SLOTS = 32
 TILE = 512
-NA = 4096
+NA = 4608
 
 
 def iota(shape, dim):
@@ -114,6 +114,9 @@
         pl.semaphore_signal(barrier, inc=1, device_id=((dp + d) % NDP, ex), device_id_type=MESH)
     for d in range(1, NEX):
         pl.semaphore_signal(barrier, inc=1, device_id=(dp, (ex + d) % NEX), device_id_type=MESH)
+    for d in range(4):
+        other = (4 - ex // 4 * 4) + d
+        pl.semaphore_signal(barrier, inc=1, device_id=(at_dp(0, 1), other), device_id_type=MESH)
 
     row = iota((256, 128), 0)
     part_of = (row & 15) >> 2
@@ -139,7 +142,7 @@
             second = jnp.concatenate([nkv_ref[0][:, :HEAD], zero, nkv_ref[0][:, HEAD:], nkv_ref[1][:, HEAD:]], axis=1)
         qs_send[t, :, 1] = by_part(dot(order, second))
 
-    pl.semaphore_wait(barrier, NDP - 1 + NEX - 1)
+    pl.semaphore_wait(barrier, NDP - 1 + NEX - 1 + 4)
 
     def spread_dp(send, recv, sems, t):
         copies = []
@@ -192,11 +195,16 @@
     want_c = 4 * (c64 >> 4) + (c64 & 3)
     weights[0].wait()
 
-    def spread_ex(send, recv, sems, t):
-        return [
-            remote(send.at[t, (ex + d) % NEX], recv.at[t, ex], sems, (t, d - 1), dp, (ex + d) % NEX)
-            for d in range(1, NEX)
-        ]
+    def crossing(other):
+        return y * 4 + (zl + other // 4 + ex // 4) % 2 * 2 + core
+
+    def spread_ex(send, recv, sems, t, nearest=True):
+        copies = []
+        for d in range(1, NEX):
+            other = (ex + d) % NEX
+            to = crossing(other) if nearest else dp
+            copies.append(remote(send.at[t, other], recv.at[t, ex], sems, (t, d - 1), to, other))
+        return copies
 
     o_copies = []
     for t in range(STEPS):
@@ -216,9 +224,10 @@
                 op_send[t, e, :, tile_at(i)] = both.astype(BF)
 
         loop(HALF // TILE, project)
-        o_copies.append(spread_ex(op_send, op_recv, o_sem, t))
-        for copy in o_copies[t]:
-            start(copy)
+        o_copies.append(spread_ex(op_send, op_recv, o_sem, t, nearest=False))
+        if t == 0:
+            for copy in o_copies[0]:
+                start(copy)
 
     d_copies = [None, None]
     targets = [None, None]
@@ -276,6 +285,9 @@
         d_copies[t] = spread_ex(ds_send, ds_recv, d_sem, t)
         for copy in d_copies[t]:
             start(copy)
+        if t == 0:
+            for copy in o_copies[1]:
+                start(copy)
 
     r_u, c_u = iota((128, 128), 0), iota((128, 128), 1)
     unfold_matrix = ones_where(((r_u >> 5) == ((c_u & 15) >> 2)) & (((r_u & 31) >> 2) == (c_u >> 4)) & ((r_u & 3) == (c_u & 3)))
@@ -545,18 +557,18 @@
     down(0, 6, 12)
     reduce_cores(0)
     gather_cross(1, 0, 1, 3)
+    gather_far(1)
+    gather_cross(1, 2)
     reduce_cross(0)
     reduce_free1(0)
-    gather_far(1)
     reduce_far(0)
+    gather_end(1)
+    gate_up(1, 0, 3)
+    reduce_bound(0, 1)
     reduce_free0(0)
-    gather_cross(1, 2)
-    gather_end(1)
-    gate_up(1, 0, 4)
-    reduce_bound(0, 1)
-    gate_up(1, 4, 8)
+    gate_up(1, 3, 9)
     reduce_bound(0, 0)
-    gate_up(1, 8, 12)
+    gate_up(1, 9, 12)
     activate(1)
     down(1, 0, 12)
     reduce_cores(1)
@@ -564,9 +576,9 @@
     reduce_cross(1)
     reduce_free1(1)
     reduce_far(1)
-    reduce_free0(1)
     finish(0)
     reduce_bound(1, 1)
+    reduce_free0(1)
     reduce_bound(1, 0)
     combine(0)
     reduce_here(1)

time: 176 us -> 163 us (0.926); the launches traced: 173 us -> 163 us
  Pallas kernels: 171 us -> 161 us
    pallas_call x1, Pallas kernels: 171 us -> 161 us  [body(): pl.pallas_call(kernel, out_shape=jax.ShapeDtypeStruct((STEPS, ROWS, D), B...]
where the time goes in v3:
time: 163 us
  Pallas kernels  161 us (99%)
    pallas_call x1, Pallas kernels, body(): pl.pallas_call(kernel, out_shape=jax.ShapeDtypeStruct((STEPS, ROWS, D), B...  161 us

profile of v3, /device:TPU:1, one launch (start us, length us, event | category | flops | bytes accessed | tf_op | source)
XLA Modules:
  0.0 162.8 jit_solution(13666454874832901222)
XLA Ops:
  0.0 161.2 %shard_map.118 = bf16[2,8,6144]{2,1,0:T(8,128)(2,1)} custom-call(bf16[2,64,384]{2,1,0:T(8,128)(2,1)} %q_ref.1, bf16[2,4,256,256]{3,2,1,0:T(8,128)(2,1)} %bitcast.11, bf16[2,64,256]{2,1,0:T(8,128)(2,1)} %bitcast.13, s32[2,64]{1,0:T(2,128)} %slot_ref.1, bf16[2,8,6144]{2,1,0:T(8,128)(2,1)} %res_ref.1, bf16[384,6144]{1,0:T(8,128)(2,1)} %wo_hbm.1, ...), custom_call_target="tpu_custom_call" | custom-call | tf_op jit(solution)/shard_map/pallas_call | solution.py:598
  161.2 1.6 copy.14

commit v4 on v3

--- a/solution.py
+++ b/solution.py
@@ -19,12 +19,15 @@
 GROUPS = 64
 D = 6144
 HALF = D // 2
-QUART = D // 4
+NC = 2048
+AB = D - NC
+QUART = AB // 4
+RAW = NC // 2 + 128
 FFD = 512
 ROWS = 8
 SLOTS = 32
 TILE = 512
-NA = 4608
+NA = 3072
 
 
 def iota(shape, dim):
@@ -60,10 +63,11 @@
 def kernel(
     q_ref, pkv_ref, nkv_ref, slot_ref, res_ref, wo_hbm, gain_ref, wr_ref, routes_ref, wg_hbm, wu_hbm, wd_hbm,
     out_ref,
-    wo, wg, wu, wd,
+    wg, wu, wd,
     qs_send, qs_recv, at_send, at_recv, op_send, op_recv, ds_send, ds_recv,
     mixed, nb, gat, held, acc_g, acc_u, hid, pair, transit, ysum, zsum, zcross, rt_send, rt_recv,
-    w_sem, q_sem, a_sem, o_sem, d_sem, g_sem, r_sem, t_sem,
+    raw_send, raw_recv, cs_send, cs_recv, cr_recv, y_send, y_recv,
+    w_sem, q_sem, a_sem, o_sem, d_sem, g_sem, r_sem, t_sem, raw_sem, dc_sem, ec_sem, y_sem,
 ):
     dp = lax.axis_index("dp")
     ex = lax.axis_index("expert")
@@ -102,6 +106,7 @@
             device_id_type=MESH,
         )
 
+    wo = pair.at[pl.ds(0, 3 * HEAD)]
     weights = [
         pltpu.make_async_copy(src, dst, w_sem.at[i])
         for i, (src, dst) in enumerate(((wo_hbm, wo), (wg_hbm, wg), (wu_hbm, wu), (wd_hbm, wd)))
@@ -217,8 +222,8 @@
         attended = dot(order, parted).astype(BF)
 
         def project(i, t=t, attended=attended):
-            lo = dot(attended, wo[:, tile_at(i)])
-            hi = dot(attended, wo[:, tile_at(i, HALF)])
+            lo = dot(attended, pair[pl.ds(0, 3 * HEAD), tile_at(i)])
+            hi = dot(attended, pair[pl.ds(0, 3 * HEAD), tile_at(i, HALF)])
             for e in range(NEX):
                 both = jnp.concatenate([lo[e * 8 : e * 8 + 8], hi[e * 8 : e * 8 + 8]], axis=0)
                 op_send[t, e, :, tile_at(i)] = both.astype(BF)
@@ -231,6 +236,8 @@
 
     d_copies = [None, None]
     targets = [None, None]
+    raw_copies = [[], []]
+    chip = dp // 2
 
     def mix(t):
         for copy in o_copies[t]:
@@ -264,9 +271,12 @@
         cols = [to_column(r) for r in rows]
         chosen = [jnp.sum(jnp.where(iota((8, 8), 1) == c, logits, 0.0), axis=1, keepdims=True) for c in cols]
         before = iota((8, 8), 1) < iota((8, 8), 0)
-        cells = []
+        cells, gates = [], []
         for k in range(2):
-            gat[t, k] = jnp.broadcast_to(jax.nn.sigmoid(chosen[k] - chosen[1 - k]), (8, 128))
+            gate = jax.nn.sigmoid(chosen[k] - chosen[1 - k])
+            gat[t, k] = jnp.broadcast_to(gate, (8, 128))
+            rounded = gate.astype(BF).astype(F32)
+            gates += [rounded, gate - rounded]
             place = jnp.zeros((8, 1), jnp.int32)
             for other in rows:
                 place = place + jnp.sum(jnp.where(before & (cols[k] == other), 1, 0), axis=1, keepdims=True)
@@ -278,13 +288,24 @@
         cell = 4 * (r_d >> 4) + (r_d & 3)
         same_quarter = ((r_d & 15) >> 2) == (c_d >> 3)
         choose = ones_where(same_quarter & ((cell_rows[0] == cell) | (cell_rows[1] == cell)))
-        quarters = jnp.concatenate([lo[:, :QUART], lo[:, QUART:], hi[:, :QUART], hi[:, QUART:]], axis=0).astype(BF)
+        quarters = jnp.concatenate([lo[:, :QUART], lo[:, QUART : 2 * QUART], lo[:, 2 * QUART :], hi[:, :QUART]], axis=0).astype(BF)
         for i in range(QUART // TILE):
             cut = slice(i * TILE, (i + 1) * TILE)
             ds_send[t, :, :, cut] = dot(choose, quarters[:, cut]).astype(BF).reshape(NEX, 16, TILE)
         d_copies[t] = spread_ex(ds_send, ds_recv, d_sem, t)
         for copy in d_copies[t]:
             start(copy)
+        lane = iota((8, 128), 1)
+        info = jnp.zeros((8, 128), F32)
+        for i, v in enumerate([c.astype(F32) for c in cells] + gates):
+            info = jnp.where(lane == i, v, info)
+        raw_send[t, :, NC // 2 :] = jnp.concatenate([info, info], axis=0).astype(BF)
+        raw_send[t, :, : NC // 2] = jnp.concatenate([hi[:, QUART : 2 * QUART], hi[:, 2 * QUART :]], axis=0).astype(BF)
+        for d in range(1, 8):
+            copy = remote(raw_send.at[t], raw_recv.at[t, chip], raw_sem, (t, d), at_dp(d // 2, d % 2), ex)
+            start(copy)
+            raw_copies[t].append(copy)
+        raw_recv[t, chip] = raw_send[t]
         if t == 0:
             for copy in o_copies[1]:
                 start(copy)
@@ -305,12 +326,63 @@
                 start = quarter * QUART + i * TILE
                 held[t, dp, :, start : start + TILE] = rows[quarter * SLOTS : (quarter + 1) * SLOTS]
 
-    part_a, part_b = pl.ds(0, NA), pl.ds(NA, D - NA)
+    zh = ex // 4
+    r256, c256 = iota((256, 256), 0), iota((256, 256), 1)
+
+    def swap(cross_of, flip_row):
+        cross = (cross_of >> 2) ^ zh
+        major, minor = r256 >> 5, (r256 & 31) >> 2
+        col_major, col_minor = c256 >> 5, (c256 & 31) >> 2
+        if flip_row:
+            same = (minor == col_major) & ((major ^ cross) == col_minor)
+        else:
+            same = (major == col_minor) & (minor == (col_major ^ cross))
+        return ones_where(same & ((r256 & 3) == (c256 & 3)))
+
+    to_chips = swap((r256 & 31) >> 2, True)
+    to_experts = swap(r256 >> 5, False)
+    dc_copies = [None, None]
+    info_of = [None, None]
+
+    def dispatch_c(t):
+        for copy in raw_copies[t]:
+            arrived(copy)
+        info = raw_recv[t, :, :, NC // 2 :].reshape(128, 128).astype(F32)
+        info_of[t] = info
+        eye = iota((128, 128), 0) == iota((128, 128), 1)
+        wanted = [jnp.sum(jnp.where(eye, info[:, k : k + 1], 0.0), axis=0, keepdims=True) for k in range(2)]
+        r, c = iota((256, 128), 0), iota((256, 128), 1)
+        cell = (4 * (r >> 5) + (r & 3)).astype(F32)
+        match = ((wanted[0] == cell) | (wanted[1] == cell)) & (((r & 31) >> 2) == (c >> 4))
+        for h in range(2):
+            choose = ones_where(match & (((c & 15) >> 3) == h))
+            for i in range(NC // 2 // TILE):
+                cut = slice(i * TILE, (i + 1) * TILE)
+                out = dot(choose, raw_recv[t, :, :, cut].reshape(128, TILE)).astype(BF)
+                cs_send[t, :, :, h * (NC // 2) + i * TILE : h * (NC // 2) + (i + 1) * TILE] = out.reshape(NEX, SLOTS, TILE)
+        dc_copies[t] = spread_ex(cs_send, cs_recv, dc_sem, t)
+        for copy in dc_copies[t]:
+            start(copy)
+        cs_recv[t, ex] = cs_send[t, ex]
+
+    def place_c(t):
+        for copy in dc_copies[t]:
+            arrived(copy)
+        for i in range(NC // TILE):
+            cut = slice(i * TILE, (i + 1) * TILE)
+            out = dot(to_chips, cs_recv[t, :, :, cut].reshape(256, TILE)).astype(BF)
+            for k in range(8):
+                held[t, k * 2 + core, :, AB + i * TILE : AB + (i + 1) * TILE] = out[k * SLOTS : (k + 1) * SLOTS]
+        for d in range(8):
+            give(t, f"last{d}", at_dp(d // 2, d % 2), at_dp(0, 0, 1), columns=part_c)
+
+    part_a, part_b = pl.ds(0, NA), pl.ds(NA, AB - NA)
+    part_ab, part_c = pl.ds(0, AB), pl.ds(AB, NC)
     whole = slice(None)
     lower, upper = pl.ds(0, 16), pl.ds(16, 16)
     g_copies = [{}, {}]
 
-    def give(t, name, device, to_dp, rows=whole, columns=whole):
+    def give(t, name, device, to_dp, rows=whole, columns=part_ab):
         ref = held.at[t, device, rows, columns]
         copy = remote(ref, ref, g_sem, (t, len(g_copies[t])), to_dp, ex)
         start(copy)
@@ -336,7 +408,7 @@
         give(t, "down1", at_dp(0, 1), at_dp(3), columns=part_a)
 
     def gather_near(t, plane):
-        columns = part_a if plane else whole
+        columns = part_a if plane else part_ab
         got(t, f"up{plane}")
         give(t, f"far_up{plane}", at_dp(3, plane), at_dp(1), lower, columns)
         got(t, f"down{plane}")
@@ -362,6 +434,9 @@
         for dy in (0, 1, 3, 2):
             got(t, f"core{dy}0", f"core{dy}1")
 
+    def gather_last(t):
+        got(t, *(f"last{d}" for d in range(8)))
+
     def gate_up(t, first, last):
         if first == 0:
             acc_g[...] = jnp.zeros_like(acc_g)
@@ -395,10 +470,16 @@
 
     def came(t, *names):
         for name in names:
-            arrived(r_copies[t][name])
+            if any(c is r_copies[t][name] for c in to_arrive):
+                arrived(r_copies[t][name])
+
+    def pair_rows(t, kind, rows=whole):
+        start, size = (0, SLOTS) if rows is whole else (rows.start, rows.size)
+        return pl.ds(pl.multiple_of((t * 8 + kind) * SLOTS + start, 16), size)
 
     def part(t, dy, plane, rows, cut):
-        return held[t, at_dp(dy, plane), rows, cut].astype(F32) + pair[t, 2 * dy + plane, rows, cut].astype(F32)
+        other = pair[pair_rows(t, 2 * dy + plane, rows), cut]
+        return held[t, at_dp(dy, plane), rows, cut].astype(F32) + other.astype(F32)
 
     def crossed(t, dy, rows, i):
         return zcross[t, dy, rows, tile_at(i)].astype(F32)
@@ -423,15 +504,16 @@
                 total = total + term(cut)
             held[t, at_dp(dy, plane), rows, cut] = total.astype(BF)
 
-        loop((D - NA) // TILE, step)
-
-    def reduce_cores(t):
+        loop((AB - NA) // TILE, step)
+
+    def reduce_cores(t, name, columns):
         for dy, plane in ((2, 1), (1, 1), (3, 1), (0, 1), (2, 0), (1, 0), (3, 0), (0, 0)):
-            kind = 2 * dy + plane
-            pass_on(t, f"core{dy}{plane}", held.at[t, at_dp(dy, plane, 1)], pair.at[t, kind], at_dp(0, 0, 1))
+            src = held.at[t, at_dp(dy, plane, 1), whole, columns]
+            dst = pair.at[pair_rows(t, 2 * dy + plane), columns]
+            pass_on(t, f"{name}{dy}{plane}", src, dst, at_dp(0, 0, 1))
 
     def send_transit(t, plane):
-        columns = part_a if plane else whole
+        columns = part_a if plane else part_ab
         for way, to_dy, rows in ((0, 1, lower), (1, 3, upper)):
             src = held.at[t, at_dp(2, plane), rows, columns]
             dst = transit.at[t, way, plane, whole, columns]
@@ -447,7 +529,7 @@
                 send_transit(t, 1)
 
     def send_sum(t, name, way, plane, rows):
-        columns = part_a if plane else whole
+        columns = part_a if plane else part_ab
         dy = 1 if way == 0 else 3
         src = held.at[t, at_dp(dy, plane), rows, columns]
         pass_on(t, f"{name}{way}{plane}", src, ysum.at[t, way, plane, rows, columns], at_dp(dy))
@@ -492,6 +574,53 @@
         came_around(t, 1)
         over_a(t, 0, 1, whole, lambda cut: around(t, 1, cut))
         pass_on(t, "z", held.at[t, at_dp(0, 1), whole, part_a], zsum.at[t], at_dp(0, 1))
+
+    ec_copies = [None, None]
+    y_copies = [[], []]
+
+    def reduce_c(t):
+        for copy in dc_copies[t]:
+            left(copy)
+        came(t, *(f"last{dy}{plane}" for dy in range(4) for plane in range(2)))
+        for i in range(NC // TILE):
+            cut = slice(AB + i * TILE, AB + (i + 1) * TILE)
+            parts = []
+            for k in range(8):
+                kind = (k // 2 + 4 - y) % 4 * 2 + (k % 2 + zl) % 2
+                total = held[t, k * 2 + core, :, cut].astype(F32) + pair[pair_rows(t, kind), cut].astype(F32)
+                parts.append(total.astype(BF))
+            out = dot(to_experts, jnp.concatenate(parts, axis=0)).astype(BF)
+            cs_send[t, :, :, i * TILE : (i + 1) * TILE] = out.reshape(NEX, SLOTS, TILE)
+        ec_copies[t] = spread_ex(cs_send, cr_recv, ec_sem, t)
+        for copy in ec_copies[t]:
+            start(copy)
+        cr_recv[t, ex] = cs_send[t, ex]
+
+    def combine_c(t):
+        for copy in ec_copies[t]:
+            arrived(copy)
+        info = raw_recv[t, :, :, NC // 2 :].reshape(128, 128).astype(F32)
+        r, c = iota((128, 256), 0), iota((128, 256), 1)
+        cell = (4 * (c >> 5) + (c & 3)).astype(F32)
+        same = ((c & 31) >> 2) == (r >> 4)
+        choose = [ones_where(same & (info[:, k : k + 1] == cell)) for k in range(2)]
+        gate = [info[:, 2 + 2 * k : 3 + 2 * k] + info[:, 3 + 2 * k : 4 + 2 * k] for k in range(2)]
+        first_half = (iota((128, TILE), 0) & 15) < 8
+
+        def both(start):
+            came_in = cr_recv[t, :, :, start : start + TILE].reshape(256, TILE)
+            return gate[0] * dot(choose[0], came_in) + gate[1] * dot(choose[1], came_in)
+
+        for i in range(NC // 2 // TILE):
+            out = jnp.where(first_half, both(i * TILE), both(NC // 2 + i * TILE)).astype(BF)
+            y_send[t, :, :, i * TILE : (i + 1) * TILE] = out.reshape(8, 16, TILE)
+        for d in range(1, 8):
+            to_y, to_z = (y + d // 2) % 4, (zl + d % 2) % 2
+            src = y_send.at[t, to_y * 2 + to_z]
+            copy = remote(src, y_recv.at[t, chip], y_sem, (t, d), at_dp(d // 2, d % 2), ex)
+            start(copy)
+            y_copies[t].append(copy)
+        y_recv[t, chip] = y_send[t, chip]
 
     t_copies = [None, None]
 
@@ -526,63 +655,92 @@
             came = rt_recv[t, :, :, i * TILE : (i + 1) * TILE].reshape(128, TILE)
             for quarter in range(4):
                 out = dot(ones_where(mine & (((c_c & 15) >> 2) == quarter)), came)
-                upper = (quarter // 2) * 8
-                start = (quarter % 2) * QUART + i * TILE
-                total = mixed[t, upper : upper + 8, start : start + TILE] + gate0 * out[:8] + gate1 * out[8:]
                 place = quarter * QUART + i * TILE
+                first, start = place // HALF * 8, place % HALF
+                total = mixed[t, first : first + 8, start : start + TILE] + gate0 * out[:8] + gate1 * out[8:]
                 out_ref[t, :, place : place + TILE] = total.astype(BF)
+
+    def combine_last(t):
+        for copy in y_copies[t]:
+            arrived(copy)
+        for i in range(NC // 2 // TILE):
+            total = jnp.zeros((16, TILE), F32)
+            for k in range(8):
+                total = total + y_recv[t, k, :, i * TILE : (i + 1) * TILE].astype(F32)
+            for h in range(2):
+                place = AB + h * (NC // 2) + i * TILE
+                both = mixed[t, 8:, place - HALF : place - HALF + TILE] + total[8 * h : 8 * h + 8]
+                out_ref[t, :, place : place + TILE] = both.astype(BF)
 
     mix(0)
     unfold(0)
     gather_own(0)
-    mix(1)
     gather_z(0)
     gather_near(0, 0)
+    mix(1)
+    dispatch_c(0)
+    gather_near(0, 1)
     unfold(1)
-    gather_near(0, 1)
     gather_own(1)
     gather_cross(0, 0, 1, 3)
     gather_far(0)
     gather_cross(0, 2)
+    dispatch_c(1)
+    gather_z(1)
     for copy in weights[1:]:
         copy.wait()
     gather_end(0)
-    gate_up(0, 0, 6)
-    gather_z(1)
-    gate_up(0, 6, 12)
+    gate_up(0, 0, 4)
     gather_near(1, 0)
+    gate_up(0, 4, 8)
+    place_c(0)
+    gather_near(1, 1)
+    gather_cross(1, 0, 1, 3)
+    gather_last(0)
+    gate_up(0, 8, 12)
+    gather_far(1)
     activate(0)
-    down(0, 0, 6)
-    gather_near(1, 1)
-    down(0, 6, 12)
-    reduce_cores(0)
-    gather_cross(1, 0, 1, 3)
-    gather_far(1)
+    down(0, 8, 12)
+    reduce_cores(0, "last", part_c)
     gather_cross(1, 2)
+    down(0, 0, 8)
+    reduce_cores(0, "core", part_ab)
+    reduce_c(0)
+    gather_end(1)
     reduce_cross(0)
     reduce_free1(0)
+    gate_up(1, 0, 2)
     reduce_far(0)
-    gather_end(1)
-    gate_up(1, 0, 3)
+    gate_up(1, 2, 5)
     reduce_bound(0, 1)
     reduce_free0(0)
-    gate_up(1, 3, 9)
+    gate_up(1, 5, 8)
+    place_c(1)
     reduce_bound(0, 0)
-    gate_up(1, 9, 12)
+    gather_last(1)
+    gate_up(1, 8, 12)
     activate(1)
-    down(1, 0, 12)
-    reduce_cores(1)
+    down(1, 8, 12)
+    reduce_cores(1, "last", part_c)
+    combine_c(0)
+    down(1, 0, 4)
     reduce_here(0)
+    reduce_c(1)
+    down(1, 4, 8)
+    reduce_cores(1, "core", part_ab)
+    finish(0)
     reduce_cross(1)
     reduce_free1(1)
     reduce_far(1)
-    finish(0)
     reduce_bound(1, 1)
     reduce_free0(1)
     reduce_bound(1, 0)
     combine(0)
+    combine_last(0)
+    combine_c(1)
     reduce_here(1)
     finish(1)
+    combine_last(1)
     combine(1)
 
     for copy in list(to_arrive):
@@ -601,7 +759,6 @@
         in_specs=[vmem] * 5 + [hbm] + [vmem] * 3 + [hbm] * 3,
         out_specs=vmem,
         scratch_shapes=[
-            pltpu.VMEM((3 * HEAD, D), BF),
             pltpu.VMEM((D, FFD), BF),
             pltpu.VMEM((D, FFD), BF),
             pltpu.VMEM((FFD, D), BF),
@@ -620,13 +777,20 @@
             pltpu.VMEM((NDP * SLOTS, FFD), F32),
             pltpu.VMEM((NDP * SLOTS, FFD), F32),
             pltpu.VMEM((NDP * SLOTS, FFD), BF),
-            pltpu.VMEM((STEPS, 8, SLOTS, D), BF),
-            pltpu.VMEM((STEPS, 2, 2, 16, D), BF),
-            pltpu.VMEM((STEPS, 2, 2, SLOTS, D), BF),
+            pltpu.VMEM((STEPS * 8 * SLOTS, D), BF),
+            pltpu.VMEM((STEPS, 2, 2, 16, AB), BF),
+            pltpu.VMEM((STEPS, 2, 2, SLOTS, AB), BF),
             pltpu.VMEM((STEPS, SLOTS, NA), BF),
-            pltpu.VMEM((STEPS, 4, SLOTS, D - NA), BF),
+            pltpu.VMEM((STEPS, 4, SLOTS, AB - NA), BF),
             pltpu.VMEM((STEPS, NEX, 16, QUART), BF),
             pltpu.VMEM((STEPS, NEX, 16, QUART), BF),
+            pltpu.VMEM((STEPS, 16, RAW), BF),
+            pltpu.VMEM((STEPS, 8, 16, RAW), BF),
+            pltpu.VMEM((STEPS, NEX, SLOTS, NC), BF),
+            pltpu.VMEM((STEPS, NEX, SLOTS, NC), BF),
+            pltpu.VMEM((STEPS, NEX, SLOTS, NC), BF),
+            pltpu.VMEM((STEPS, 8, 16, NC // 2), BF),
+            pltpu.VMEM((STEPS, 8, 16, NC // 2), BF),
             dma((4,)),
             dma((2, STEPS, NDP - 1)),
             dma((2, STEPS, NDP - 1)),
@@ -635,6 +799,10 @@
             dma((2, STEPS, 40)),
             dma((2, STEPS, 40)),
             dma((2, STEPS, NEX - 1)),
+            dma((2, STEPS, 8)),
+            dma((2, STEPS, NEX - 1)),
+            dma((2, STEPS, NEX - 1)),
+            dma((2, STEPS, 8)),
         ],
         compiler_params=pltpu.CompilerParams(
             collective_id=0, has_side_effects=True, vmem_limit_bytes=63 * 1024 * 1024

time: 163 us -> 152 us (0.933)
  Pallas kernels: 161 us -> 149 us
    pallas_call x1, Pallas kernels: 161 us -> 149 us  [body(): pl.pallas_call(kernel, out_shape=jax.ShapeDtypeStruct((STEPS, ROWS, D), B...]
where the time goes in v4:
time: 152 us; the launch traced here: 150 us
  Pallas kernels  149 us (98%)
  local copies, waits for them, and re-layouts  1.62 us (1%)
    pallas_call x1, Pallas kernels, body(): pl.pallas_call(kernel, out_shape=jax.ShapeDtypeStruct((STEPS, ROWS, D), B...  149 us

profile of v4, /device:TPU:1, one launch (start us, length us, event | category | flops | bytes accessed | tf_op | source)
XLA Modules:
  0.0 150.5 jit_solution(15693970479857810393)
XLA Ops:
  0.0 148.9 %shard_map.118 = bf16[2,8,6144]{2,1,0:T(8,128)(2,1)} custom-call(bf16[2,64,384]{2,1,0:T(8,128)(2,1)} %q_ref.1, bf16[2,4,256,256]{3,2,1,0:T(8,128)(2,1)} %bitcast.11, bf16[2,64,256]{2,1,0:T(8,128)(2,1)} %bitcast.13, s32[2,64]{1,0:T(2,128)} %slot_ref.1, bf16[2,8,6144]{2,1,0:T(8,128)(2,1)} %res_ref.1, bf16[384,6144]{1,0:T(8,128)(2,1)} %wo_hbm.1, ...), custom_call_target="tpu_custom_call" | custom-call | tf_op jit(solution)/shard_map/pallas_call | solution.py:756
  148.9 1.6 %copy.14 = bf16[2,8,6144]{2,1,0:T(8,128)(2,1)} copy(bf16[2,8,6144]{2,1,0:T(8,128)(2,1)} %shard_map.118) | data formatting | bytes 393216

commit v5 on v4

--- a/solution.py
+++ b/solution.py
@@ -722,22 +722,22 @@
     activate(1)
     down(1, 8, 12)
     reduce_cores(1, "last", part_c)
-    combine_c(0)
     down(1, 0, 4)
     reduce_here(0)
     reduce_c(1)
     down(1, 4, 8)
     reduce_cores(1, "core", part_ab)
-    finish(0)
     reduce_cross(1)
     reduce_free1(1)
     reduce_far(1)
+    combine_c(0)
     reduce_bound(1, 1)
     reduce_free0(1)
     reduce_bound(1, 0)
+    finish(0)
+    combine_c(1)
     combine(0)
     combine_last(0)
-    combine_c(1)
     reduce_here(1)
     finish(1)
     combine_last(1)

time: 152 us -> 151 us (level)
  no operation moved by 1% of the time
where the time goes in v5:
time: 151 us; the launch traced here: 149 us
  Pallas kernels  148 us (98%)
  local copies, waits for them, and re-layouts  1.62 us (1%)
    pallas_call x1, Pallas kernels, body(): pl.pallas_call(kernel, out_shape=jax.ShapeDtypeStruct((STEPS, ROWS, D), B...  148 us

profile of v5, /device:TPU:1, one launch (start us, length us, event | category | flops | bytes accessed | tf_op | source)
XLA Modules:
  0.0 149.3 jit_solution(15105810133424814899)
XLA Ops:
  0.0 147.7 %shard_map.118 = bf16[2,8,6144]{2,1,0:T(8,128)(2,1)} custom-call(bf16[2,64,384]{2,1,0:T(8,128)(2,1)} %q_ref.1, bf16[2,4,256,256]{3,2,1,0:T(8,128)(2,1)} %bitcast.11, bf16[2,64,256]{2,1,0:T(8,128)(2,1)} %bitcast.13, s32[2,64]{1,0:T(2,128)} %slot_ref.1, bf16[2,8,6144]{2,1,0:T(8,128)(2,1)} %res_ref.1, bf16[384,6144]{1,0:T(8,128)(2,1)} %wo_hbm.1, ...), custom_call_target="tpu_custom_call" | custom-call | tf_op jit(solution)/shard_map/pallas_call | solution.py:756
  147.7 1.6 %copy.14 = bf16[2,8,6144]{2,1,0:T(8,128)(2,1)} copy(bf16[2,8,6144]{2,1,0:T(8,128)(2,1)} %shard_map.118) | data formatting | bytes 393216

commit v6 on v5

--- a/solution.py
+++ b/solution.py
@@ -723,8 +723,8 @@
     down(1, 8, 12)
     reduce_cores(1, "last", part_c)
     down(1, 0, 4)
+    reduce_c(1)
     reduce_here(0)
-    reduce_c(1)
     down(1, 4, 8)
     reduce_cores(1, "core", part_ab)
     reduce_cross(1)

time: 151 us -> 151 us (level)
  Pallas kernels: 148 us -> 146 us
where the time goes in v6:
time: 151 us; the launch traced here: 148 us
  Pallas kernels  146 us (97%)
  local copies, waits for them, and re-layouts  1.62 us (1%)
    pallas_call x1, Pallas kernels, body(): pl.pallas_call(kernel, out_shape=jax.ShapeDtypeStruct((STEPS, ROWS, D), B...  146 us

profile of v6, /device:TPU:1, one launch (start us, length us, event | category | flops | bytes accessed | tf_op | source)
XLA Modules:
  0.0 148.1 jit_solution(3989873428917229873)
XLA Ops:
  0.0 146.5 %shard_map.118 = bf16[2,8,6144]{2,1,0:T(8,128)(2,1)} custom-call(bf16[2,64,384]{2,1,0:T(8,128)(2,1)} %q_ref.1, bf16[2,4,256,256]{3,2,1,0:T(8,128)(2,1)} %bitcast.11, bf16[2,64,256]{2,1,0:T(8,128)(2,1)} %bitcast.13, s32[2,64]{1,0:T(2,128)} %slot_ref.1, bf16[2,8,6144]{2,1,0:T(8,128)(2,1)} %res_ref.1, bf16[384,6144]{1,0:T(8,128)(2,1)} %wo_hbm.1, ...), custom_call_target="tpu_custom_call" | custom-call | tf_op jit(solution)/shard_map/pallas_call | solution.py:756
  146.5 1.6 %copy.14 = bf16[2,8,6144]{2,1,0:T(8,128)(2,1)} copy(bf16[2,8,6144]{2,1,0:T(8,128)(2,1)} %shard_map.118) | data formatting | bytes 393216
